TPU v7x, 32 devices: a whole 2x2x4 slice. The times are simulated.
32 devices in a mesh: group: 2 (over y), dp: 8 (over z, x), tensor: 2 (over core).
Axes of the slice: x: 2, y: 2, z: 4, core: 2. Of those that a mesh axis runs over, the one named last changes fastest.
Arguments:
- layer_input: bfloat16 [2, 16, 512, 768], P(None, ('group', 'dp'), 'tensor'), may hold values from -6 to 6
- out_cotangent: bfloat16 [2, 16, 512, 768], P(None, ('group', 'dp'), 'tensor'), may hold values from -6 to 6
- lengths: int32 [2, 16], P(None, ('group', 'dp')), may hold values from 128 to 512, as said below
- global_blocks: int32 [2, 16, 2], P(None, ('group', 'dp')), may hold values from 0 to 7, as said below
- rand_blocks: int32 [2, 16, 8, 12, 3], P(None, ('group', 'dp'), None, 'tensor'), may hold values from 0 to 7, as said below
- inner_steps: int32 [2], P('group'), may hold values from 1 to 20
- wide_inner: float32 [2, 1, 768, 2, 2688], P('group', None, 'dp', 'tensor'), may hold values from -0.21875 to 0.21875
- wide_first: float32 [2, 1, 768, 2, 2688], P('group', None, 'dp', 'tensor'), may hold values from -19.00703 to 19.00703
- wide_second: float32 [2, 1, 768, 2, 2688], P('group', None, 'dp', 'tensor'), may hold values from 0.8192 to 8.192
- wide_anchor: float32 [1, 768, 2, 2688], P(None, 'dp', 'tensor'), may hold values from -0.21875 to 0.21875
- wide_outer: float32 [1, 768, 2, 2688], P(None, 'dp', 'tensor'), may hold values from -0.06 to 0.06
- narrow_inner: float32 [2, 1, 2, 1920, 768], P('group', None, 'tensor', 'dp'), may hold values from -0.21875 to 0.21875
- narrow_first: float32 [2, 1, 2, 1920, 768], P('group', None, 'tensor', 'dp'), may hold values from -19.00703 to 19.00703
- narrow_second: float32 [2, 1, 2, 1920, 768], P('group', None, 'tensor', 'dp'), may hold values from 0.8192 to 8.192
- narrow_anchor: float32 [1, 2, 1920, 768], P(None, 'tensor', 'dp'), may hold values from -0.21875 to 0.21875
- narrow_outer: float32 [1, 2, 1920, 768], P(None, 'tensor', 'dp'), may hold values from -0.06 to 0.06
- bias_inner: float32 [2, 1, 2, 2304], P('group', None, 'tensor', 'dp'), may hold values from -3 to 3
- bias_first: float32 [2, 1, 2, 2304], P('group', None, 'tensor', 'dp'), may hold values from -19.00703 to 19.00703
- bias_second: float32 [2, 1, 2, 2304], P('group', None, 'tensor', 'dp'), may hold values from 0.8192 to 8.192
- bias_anchor: float32 [1, 2, 2304], P(None, 'tensor', 'dp'), may hold values from -3 to 3
- bias_outer: float32 [1, 2, 2304], P(None, 'tensor', 'dp'), may hold values from -0.06 to 0.06
- norms_inner: float32 [2, 1, 6, 768], P('group', None, None, ('dp', 'tensor')), may hold values from 0.5 to 1.5
- norms_first: float32 [2, 1, 6, 768], P('group', None, None, ('dp', 'tensor')), may hold values from -19.00703 to 19.00703
- norms_second: float32 [2, 1, 6, 768], P('group', None, None, ('dp', 'tensor')), may hold values from 0.8192 to 8.192
- norms_anchor: float32 [1, 6, 768], P(None, None, ('dp', 'tensor')), may hold values from 0.5 to 1.5
- norms_outer: float32 [1, 6, 768], P(None, None, ('dp', 'tensor')), may hold values from -0.06 to 0.06
Outputs:
- layer_out: float32 [2, 16, 512, 768], P(None, ('group', 'dp'), 'tensor')
- input_grad: float32 [2, 16, 512, 768], P(None, ('group', 'dp'), 'tensor')
- wide_grad: float32 [2, 1, 768, 2, 2688], P('group', None, 'dp', 'tensor')
- wide_first_new: float32 [2, 1, 768, 2, 2688], P('group', None, 'dp', 'tensor')
- wide_second_new: float32 [2, 1, 768, 2, 2688], P('group', None, 'dp', 'tensor')
- wide_mean_diff: float32 [1, 768, 2, 2688], P(None, 'dp', 'tensor')
- wide_outer_new: float32 [1, 768, 2, 2688], P(None, 'dp', 'tensor')
- wide_anchor_new: float32 [1, 768, 2, 2688], P(None, 'dp', 'tensor')
- narrow_grad: float32 [2, 1, 2, 1920, 768], P('group', None, 'tensor', 'dp')
- narrow_first_new: float32 [2, 1, 2, 1920, 768], P('group', None, 'tensor', 'dp')
- narrow_second_new: float32 [2, 1, 2, 1920, 768], P('group', None, 'tensor', 'dp')
- narrow_mean_diff: float32 [1, 2, 1920, 768], P(None, 'tensor', 'dp')
- narrow_outer_new: float32 [1, 2, 1920, 768], P(None, 'tensor', 'dp')
- narrow_anchor_new: float32 [1, 2, 1920, 768], P(None, 'tensor', 'dp')
- bias_grad: float32 [2, 1, 2, 2304], P('group', None, 'tensor', 'dp')
- bias_first_new: float32 [2, 1, 2, 2304], P('group', None, 'tensor', 'dp')
- bias_second_new: float32 [2, 1, 2, 2304], P('group', None, 'tensor', 'dp')
- bias_mean_diff: float32 [1, 2, 2304], P(None, 'tensor', 'dp')
- bias_outer_new: float32 [1, 2, 2304], P(None, 'tensor', 'dp')
- bias_anchor_new: float32 [1, 2, 2304], P(None, 'tensor', 'dp')
- norms_grad: float32 [2, 1, 6, 768], P('group', None, None, ('dp', 'tensor'))
- norms_first_new: float32 [2, 1, 6, 768], P('group', None, None, ('dp', 'tensor'))
- norms_second_new: float32 [2, 1, 6, 768], P('group', None, None, ('dp', 'tensor'))
- norms_mean_diff: float32 [1, 6, 768], P(None, None, ('dp', 'tensor'))
- norms_outer_new: float32 [1, 6, 768], P(None, None, ('dp', 'tensor'))
- norms_anchor_new: float32 [1, 6, 768], P(None, None, ('dp', 'tensor'))
Inputs may be any that keep to these rules, and one draw needn't show every extreme that they name: `lengths`: slot 0 of every micro-batch is full. `global_blocks`: two different blocks per sequence, both holding real tokens. `rand_blocks`: for each block row and head, three different blocks, none within one block of the row and none of the sequence's global blocks.
All inputs are finite; a program needn't handle non-finite values.
Results may differ from a plain program's by a relative error of at most 0.0095.
The roundings to bfloat16 on the way count: a program that leaves them out, or rounds other values in their place, can miss the bound.
Values may be sent and summed in bfloat16 or wider, within the bound.
A program may use at most 192 MiB of HBM per device.

v0:
```python
import jax
import jax.numpy as jnp
from jax import lax
from jax.sharding import PartitionSpec as P

BETA_ONE = 0.9
BETA_TWO = 0.99
ADAM_EPS = 1e-08
LEARN_RATE = 0.04
DECAY_RATE = 0.1
OUTER_BETA = 0.9
OUTER_RATE = 0.7
NORM_EPS = 1e-06
MASKED = -1e30


def gelu_tanh(values):
    return jax.nn.gelu(values, approximate=True)


def norm_stats(values):
    average = jnp.mean(values, axis=-1, keepdims=True)
    centred = values - average
    spread = jnp.mean(centred * centred, axis=-1, keepdims=True)
    scaling = lax.rsqrt(spread + NORM_EPS)
    return (centred * scaling, scaling)


def norm_back(grad_rows, normed, scaling, gain):
    scaled = grad_rows * gain
    return scaling * (
        scaled
        - jnp.mean(scaled, axis=-1, keepdims=True)
        - normed * jnp.mean(scaled * normed, axis=-1, keepdims=True)
    )


def rows_forward(values):
    return lax.all_gather(values, "tensor", axis=0, tiled=True)


def sum_forward(values):
    return lax.psum_scatter(values, "tensor", scatter_dimension=0, tiled=True)


def rows_backward(values):
    return lax.all_gather(values, "tensor", axis=0, tiled=True)


def sum_backward(values):
    return lax.psum_scatter(values, "tensor", scatter_dimension=0, tiled=True)


def block_mask(global_pair, random_rows, block_total):
    block_ids = jnp.arange(block_total, dtype=jnp.int32)
    nearby = jnp.abs(block_ids[:, None] - block_ids[None, :]) <= 1
    global_hit = jnp.any(block_ids[:, None] == global_pair[None, :], axis=1)
    allowed_base = nearby | global_hit[None, :] | global_hit[:, None]
    chosen = jnp.any(
        jnp.transpose(random_rows, (1, 0, 2))[:, :, None, :] == block_ids[None, None, :, None],
        axis=3,
    )
    return allowed_base[None] | chosen


def split_blocks(blocks_ok, seq_len, block_len):
    heads_dev = blocks_ok.shape[0]
    query_rows = min(seq_len, 512)
    block_count = seq_len // query_rows
    per_rows = query_rows // block_len
    mask_parts = jnp.transpose(
        blocks_ok.reshape(heads_dev, block_count, per_rows, -1), (1, 0, 2, 3)
    )
    return (mask_parts, query_rows, block_count)


def attend_forward(queries, keys_all, values_all, blocks_ok, key_ok, block_len):
    seq_len, heads_dev, head_width = queries.shape
    scaling = head_width ** (-0.5)
    mask_parts, query_rows, block_count = split_blocks(blocks_ok, seq_len, block_len)
    query_parts = queries.reshape(block_count, query_rows, heads_dev, head_width)

    def per_block(operands):
        query_part, mask_part = operands
        allowed = (
            jnp.repeat(jnp.repeat(mask_part, block_len, axis=1), block_len, axis=2)
            & key_ok[None, None, :]
        )
        scores = (
            jnp.einsum("qhd,khd->hqk", query_part, keys_all, preferred_element_type=jnp.float32)
            * scaling
        )
        masked = jnp.where(allowed, scores, MASKED)
        highest = jnp.max(masked, axis=2, keepdims=True)
        weights_exp = jnp.exp(masked - highest)
        summed = jnp.sum(weights_exp, axis=2, keepdims=True)
        prob_rows = (weights_exp / summed).astype(jnp.bfloat16)
        outputs = jnp.einsum(
            "hqk,khd->qhd", prob_rows, values_all, preferred_element_type=jnp.float32
        )
        return (outputs, (highest + jnp.log(summed))[:, :, 0])

    outputs, log_totals = lax.map(per_block, (query_parts, mask_parts))
    return (outputs.reshape(seq_len, heads_dev * head_width), log_totals)


def attend_backward(
    queries, keys_all, values_all, grad_mixed, log_totals, blocks_ok, key_ok, block_len
):
    seq_len, heads_dev, head_width = queries.shape
    scaling = head_width ** (-0.5)
    mask_parts, query_rows, block_count = split_blocks(blocks_ok, seq_len, block_len)
    query_parts = queries.reshape(block_count, query_rows, heads_dev, head_width)
    grad_parts = grad_mixed.reshape(block_count, query_rows, heads_dev, head_width)

    def per_block(running, operands):
        key_total, value_total = running
        query_part, mask_part, grad_part, total_part = operands
        allowed = (
            jnp.repeat(jnp.repeat(mask_part, block_len, axis=1), block_len, axis=2)
            & key_ok[None, None, :]
        )
        scores = (
            jnp.einsum("qhd,khd->hqk", query_part, keys_all, preferred_element_type=jnp.float32)
            * scaling
        )
        prob_rows = jnp.exp(jnp.where(allowed, scores, MASKED) - total_part[:, :, None])
        grad_probs = jnp.einsum(
            "qhd,khd->hqk", grad_part, values_all, preferred_element_type=jnp.float32
        )
        centre = jnp.sum(prob_rows * grad_probs, axis=2, keepdims=True)
        grad_scores = (prob_rows * (grad_probs - centre)).astype(jnp.bfloat16)
        query_grad = (
            jnp.einsum("hqk,khd->qhd", grad_scores, keys_all, preferred_element_type=jnp.float32)
            * scaling
        )
        key_total = (
            key_total
            + jnp.einsum(
                "hqk,qhd->khd", grad_scores, query_part, preferred_element_type=jnp.float32
            )
            * scaling
        )
        value_total = value_total + jnp.einsum(
            "hqk,qhd->khd",
            prob_rows.astype(jnp.bfloat16),
            grad_part,
            preferred_element_type=jnp.float32,
        )
        return ((key_total, value_total), query_grad)

    zeros_init = jnp.zeros(keys_all.shape, jnp.float32)
    (key_grad, value_grad), query_grad = lax.scan(
        per_block, (zeros_init, zeros_init), (query_parts, mask_parts, grad_parts, log_totals)
    )
    flat = heads_dev * head_width
    return (
        query_grad.reshape(seq_len, flat),
        key_grad.reshape(seq_len, flat),
        value_grad.reshape(seq_len, flat),
    )


def adam_step(weight, gradient, first, second, count):
    first_new = BETA_ONE * first + (1.0 - BETA_ONE) * gradient
    second_new = BETA_TWO * second + (1.0 - BETA_TWO) * gradient * gradient
    first_hat = first_new / (1.0 - BETA_ONE**count)
    second_hat = second_new / (1.0 - BETA_TWO**count)
    weight_new = weight - LEARN_RATE * (
        first_hat / (jnp.sqrt(second_hat) + ADAM_EPS) + DECAY_RATE * weight
    )
    return (weight_new, first_new, second_new)


def on_device(
    layer_input,
    out_cotangent,
    lengths,
    global_blocks,
    rand_blocks,
    inner_steps,
    wide_inner,
    wide_first,
    wide_second,
    wide_anchor,
    wide_outer,
    narrow_inner,
    narrow_first,
    narrow_second,
    narrow_anchor,
    narrow_outer,
    bias_inner,
    bias_first,
    bias_second,
    bias_anchor,
    bias_outer,
    norms_inner,
    norms_first,
    norms_second,
    norms_anchor,
    norms_outer,
):
    micro_count = layer_input.shape[0]
    row_count = layer_input.shape[2]
    layers = wide_inner.shape[1]
    tensor_count = lax.axis_size("tensor")
    seq_len = row_count * tensor_count
    block_total = rand_blocks.shape[2]
    block_len = seq_len // block_total
    heads_dev = rand_blocks.shape[3]
    model_width = layer_input.shape[3]
    head_width = model_width // (heads_dev * tensor_count)
    attn_cols = heads_dev * head_width
    own_rows = lax.axis_index("tensor") * row_count + jnp.arange(row_count, dtype=jnp.int32)
    norms_full = lax.all_gather(
        norms_inner[0].astype(jnp.bfloat16), ("dp", "tensor"), axis=2, tiled=True
    ).astype(jnp.float32)
    outs_rows = []
    grads_rows = []
    collected = []
    collected_rows = []
    for micro_index in range(micro_count):
        weights = [
            (
                lax.all_gather(
                    wide_inner[0, 0, :, 0, :].astype(jnp.bfloat16), "dp", axis=0, tiled=True
                ),
                lax.all_gather(
                    narrow_inner[0, 0, 0].astype(jnp.bfloat16), "dp", axis=0, tiled=True
                ),
                lax.all_gather(bias_inner[0, 0, 0].astype(jnp.bfloat16), "dp", axis=0, tiled=True),
            )
        ]
        length = lengths[micro_index, 0]
        key_ok = jnp.arange(seq_len, dtype=jnp.int32) < length
        row_ok = (own_rows < length).astype(jnp.float32)[:, None]
        blocks_ok = block_mask(
            global_blocks[micro_index, 0], rand_blocks[micro_index, 0], block_total
        )
        hidden = layer_input[micro_index, 0].astype(jnp.float32)
        layer_index = 0
        w_wide, w_narrow, w_bias = weights[layer_index]
        bias_rows = w_bias.astype(jnp.float32)
        norm_rows = norms_full[layer_index]
        inputs_one = rows_forward(hidden.astype(jnp.bfloat16))
        qkv_bias = jnp.concatenate(
            [
                bias_rows[:attn_cols],
                jnp.zeros((attn_cols,), jnp.float32),
                bias_rows[attn_cols : 2 * attn_cols],
            ]
        )
        qkv = (
            jnp.dot(inputs_one, w_wide[:, : 3 * attn_cols], preferred_element_type=jnp.float32)
            + qkv_bias
        ).astype(jnp.bfloat16)
        queries = qkv[:, :attn_cols].reshape(seq_len, heads_dev, head_width)
        keys_all = qkv[:, attn_cols : 2 * attn_cols].reshape(seq_len, heads_dev, head_width)
        values_all = qkv[:, 2 * attn_cols :].reshape(seq_len, heads_dev, head_width)
        mixed, log_totals = attend_forward(
            queries, keys_all, values_all, blocks_ok, key_ok, block_len
        )
        mixed = mixed.astype(jnp.bfloat16)
        branch = sum_forward(
            jnp.dot(mixed, w_narrow[:attn_cols], preferred_element_type=jnp.float32)
        )
        normed, scaling = norm_stats(hidden + branch + norm_rows[0])
        first_out = normed * norm_rows[2] + norm_rows[3]
        inputs_two = rows_forward(first_out.astype(jnp.bfloat16))
        inner_pre = (
            jnp.dot(inputs_two, w_wide[:, 3 * attn_cols :], preferred_element_type=jnp.float32)
            + bias_rows[2 * attn_cols :]
        )
        gelu_vals, gelu_pull = jax.vjp(gelu_tanh, inner_pre)
        gelu_out = gelu_vals.astype(jnp.bfloat16)
        branch_two = sum_forward(
            jnp.dot(gelu_out, w_narrow[attn_cols:], preferred_element_type=jnp.float32)
        )
        normed_two, scaling_two = norm_stats(first_out + branch_two + norm_rows[1])
        stored = [
            (
                inputs_one,
                queries,
                keys_all,
                values_all,
                mixed,
                log_totals,
                normed,
                scaling,
                inputs_two,
                gelu_pull,
                gelu_out,
                normed_two,
                scaling_two,
            )
        ]
        hidden = normed_two * norm_rows[4] + norm_rows[5]
        outs_rows.append(hidden)
        grad_rows = out_cotangent[micro_index, 0].astype(jnp.float32) * row_ok
        pieces = [None] * layers
        for layer_index in reversed(range(layers)):
            (
                inputs_one,
                queries,
                keys_all,
                values_all,
                mixed,
                log_totals,
                normed,
                scaling,
                inputs_two,
                gelu_pull,
                gelu_out,
                normed_two,
                scaling_two,
            ) = stored[layer_index]
            w_wide, w_narrow, w_bias = weights[layer_index]
            norm_rows = norms_full[layer_index]
            gain_two_grad = jnp.sum(grad_rows * normed_two, axis=0)
            shift_two_grad = jnp.sum(grad_rows, axis=0)
            residual_two = norm_back(grad_rows, normed_two, scaling_two, norm_rows[4])
            down_bias_grad = jnp.sum(residual_two, axis=0)
            full_two = rows_backward(residual_two.astype(jnp.bfloat16))
            down_grad = jnp.einsum(
                "sf,sd->fd", gelu_out, full_two, preferred_element_type=jnp.float32
            )
            gelu_grad = jnp.einsum(
                "sd,fd->sf", full_two, w_narrow[attn_cols:], preferred_element_type=jnp.float32
            )
            inner_grad = gelu_pull(gelu_grad)[0].astype(jnp.bfloat16)
            up_bias_grad = jnp.sum(inner_grad, axis=0, dtype=jnp.float32)
            up_grad = jnp.einsum(
                "sd,sf->df", inputs_two, inner_grad, preferred_element_type=jnp.float32
            )
            first_grad = residual_two + sum_backward(
                jnp.einsum(
                    "sf,df->sd",
                    inner_grad,
                    w_wide[:, 3 * attn_cols :],
                    preferred_element_type=jnp.float32,
                )
            )
            gain_one_grad = jnp.sum(first_grad * normed, axis=0)
            shift_one_grad = jnp.sum(first_grad, axis=0)
            residual_one = norm_back(first_grad, normed, scaling, norm_rows[2])
            out_bias_grad = jnp.sum(residual_one, axis=0)
            full_one = rows_backward(residual_one.astype(jnp.bfloat16))
            out_grad = jnp.einsum("sa,sd->ad", mixed, full_one, preferred_element_type=jnp.float32)
            mixed_grad = jnp.einsum(
                "sd,ad->sa", full_one, w_narrow[:attn_cols], preferred_element_type=jnp.float32
            ).astype(jnp.bfloat16)
            query_grad, key_grad, value_grad = attend_backward(
                queries,
                keys_all,
                values_all,
                mixed_grad.reshape(seq_len, heads_dev, head_width),
                log_totals,
                blocks_ok,
                key_ok,
                block_len,
            )
            qkv_grad = jnp.concatenate([query_grad, key_grad, value_grad], axis=1).astype(
                jnp.bfloat16
            )
            query_bias_grad = jnp.sum(qkv_grad[:, :attn_cols], axis=0, dtype=jnp.float32)
            value_bias_grad = jnp.sum(qkv_grad[:, 2 * attn_cols :], axis=0, dtype=jnp.float32)
            attn_weight_grad = jnp.einsum(
                "sd,sc->dc", inputs_one, qkv_grad, preferred_element_type=jnp.float32
            )
            grad_rows = residual_one + sum_backward(
                jnp.einsum(
                    "sc,dc->sd",
                    qkv_grad,
                    w_wide[:, : 3 * attn_cols],
                    preferred_element_type=jnp.float32,
                )
            )
            pieces[layer_index] = (
                jnp.concatenate([attn_weight_grad, up_grad], axis=1),
                jnp.concatenate([out_grad, down_grad], axis=0),
                jnp.concatenate([query_bias_grad, value_bias_grad, up_bias_grad]),
                jnp.stack(
                    [
                        out_bias_grad,
                        down_bias_grad,
                        gain_one_grad,
                        shift_one_grad,
                        gain_two_grad,
                        shift_two_grad,
                    ]
                ),
            )
        grads_rows.append(grad_rows)
        micro_pieces = (
            jnp.stack([item[0] for item in pieces]),
            jnp.stack([item[1] for item in pieces]),
            jnp.stack([item[2] for item in pieces]),
        )
        collected_rows.append(jnp.stack([item[3] for item in pieces]))
        collected.append(micro_pieces)
    merged = collected[0]
    for extra in collected[1:]:
        merged = jax.tree.map(jnp.add, merged, extra)
    merged_rows = collected_rows[0]
    for extra in collected_rows[1:]:
        merged_rows = merged_rows + extra
    shards = (
        lax.psum_scatter(merged[0], "dp", scatter_dimension=1, tiled=True),
        lax.psum_scatter(merged[1], "dp", scatter_dimension=1, tiled=True),
        lax.psum_scatter(merged[2], "dp", scatter_dimension=1, tiled=True),
    )
    row_shard = lax.psum_scatter(merged_rows, ("dp", "tensor"), scatter_dimension=2, tiled=True)
    grads = (
        shards[0][None, :, :, None, :],
        shards[1][None, :, None],
        shards[2][None, :, None],
        row_shard[None],
    )
    inners = (wide_inner, narrow_inner, bias_inner, norms_inner)
    firsts = (wide_first, narrow_first, bias_first, norms_first)
    seconds = (wide_second, narrow_second, bias_second, norms_second)
    anchors = (wide_anchor, narrow_anchor, bias_anchor, norms_anchor)
    outers = (wide_outer, narrow_outer, bias_outer, norms_outer)
    count = inner_steps[0].astype(jnp.float32)
    updated = [
        adam_step(inners[kind], grads[kind], firsts[kind], seconds[kind], count)
        for kind in range(4)
    ]
    diffs = tuple((anchors[kind] - updated[kind][0][0] for kind in range(4)))
    diff_sums = lax.psum((diffs[0], diffs[1], diffs[2], diffs[3]), "group")
    group_count = lax.axis_size("group")
    results = []
    for kind in range(4):
        mean_diff = diff_sums[kind] / group_count
        outer_new = OUTER_BETA * outers[kind] + mean_diff
        anchor_new = anchors[kind] - OUTER_RATE * (mean_diff + OUTER_BETA * outer_new)
        results.append(
            (grads[kind], updated[kind][1], updated[kind][2], mean_diff, outer_new, anchor_new)
        )
    layer_out = jnp.stack(outs_rows)[:, None]
    input_grad = jnp.stack(grads_rows)[:, None]
    return (
        layer_out,
        input_grad,
        results[0][0],
        results[0][1],
        results[0][2],
        results[0][3],
        results[0][4],
        results[0][5],
        results[1][0],
        results[1][1],
        results[1][2],
        results[1][3],
        results[1][4],
        results[1][5],
        results[2][0],
        results[2][1],
        results[2][2],
        results[2][3],
        results[2][4],
        results[2][5],
        results[3][0],
        results[3][1],
        results[3][2],
        results[3][3],
        results[3][4],
        results[3][5],
    )


def solution(mesh):
    return jax.shard_map(
        on_device,
        mesh=mesh,
        in_specs=(
            P(None, ("group", "dp"), "tensor", None),
            P(None, ("group", "dp"), "tensor", None),
            P(None, ("group", "dp")),
            P(None, ("group", "dp"), None),
            P(None, ("group", "dp"), None, "tensor", None),
            P("group"),
            P("group", None, "dp", "tensor", None),
            P("group", None, "dp", "tensor", None),
            P("group", None, "dp", "tensor", None),
            P(None, "dp", "tensor", None),
            P(None, "dp", "tensor", None),
            P("group", None, "tensor", "dp", None),
            P("group", None, "tensor", "dp", None),
            P("group", None, "tensor", "dp", None),
            P(None, "tensor", "dp", None),
            P(None, "tensor", "dp", None),
            P("group", None, "tensor", "dp"),
            P("group", None, "tensor", "dp"),
            P("group", None, "tensor", "dp"),
            P(None, "tensor", "dp"),
            P(None, "tensor", "dp"),
            P("group", None, None, ("dp", "tensor")),
            P("group", None, None, ("dp", "tensor")),
            P("group", None, None, ("dp", "tensor")),
            P(None, None, ("dp", "tensor")),
            P(None, None, ("dp", "tensor")),
        ),
        out_specs=(
            P(None, ("group", "dp"), "tensor", None),
            P(None, ("group", "dp"), "tensor", None),
            P("group", None, "dp", "tensor", None),
            P("group", None, "dp", "tensor", None),
            P("group", None, "dp", "tensor", None),
            P(None, "dp", "tensor", None),
            P(None, "dp", "tensor", None),
            P(None, "dp", "tensor", None),
            P("group", None, "tensor", "dp", None),
            P("group", None, "tensor", "dp", None),
            P("group", None, "tensor", "dp", None),
            P(None, "tensor", "dp", None),
            P(None, "tensor", "dp", None),
            P(None, "tensor", "dp", None),
            P("group", None, "tensor", "dp"),
            P("group", None, "tensor", "dp"),
            P("group", None, "tensor", "dp"),
            P(None, "tensor", "dp"),
            P(None, "tensor", "dp"),
            P(None, "tensor", "dp"),
            P("group", None, None, ("dp", "tensor")),
            P("group", None, None, ("dp", "tensor")),
            P("group", None, None, ("dp", "tensor")),
            P(None, None, ("dp", "tensor")),
            P(None, None, ("dp", "tensor")),
            P(None, None, ("dp", "tensor")),
        ),
        check_vma=False,
    )
```

profile of v0, /device:TPU:0, one launch (start us, length us, event | category | flops | bytes accessed | tf_op | source)
XLA Modules:
  0.0 791.7 jit_solution(1354002547229199632)
XLA Ops:
  7.3 2.1 copy.338
  9.5 1.9 convert_element_type.195
  13.0 23.8 %all-reduce = bf16[2304]{0:T(1024)(128)(2,1)S(1)} all-reduce(bf16[2304]{0:T(1024)(128)(2,1)S(1)} %dynamic-update-slice), channel_id=4, replica_groups=mesh['group'=2,'dp'=8,'tensor'=2] {'dp'}, use_global_device_ids=true, to_apply=%add | all-reduce | flops 2304 | bytes 9216
  38.9 2.4 all-gather
  41.2 45.3 %all-gather.9.cloned.1.call-done = bf16[1,1,768,1,2688]{4,2,3,1,0:T(8,128)(2,1)} async-done(((bf16[1,1,96,1,2688]{4,2,3,1,0:T(8,128)(2,1)}), bf16[1,1,768,1,2688]{4,2,3,1,0:T(8,128)(2,1)}) %all-gather.9.cloned.1.call-update) | async-done | bytes 4128784 | tf_op jit(solution)/shard_map/all_gather | solution.py:225
  86.6 2.7 fusion.26
  95.6 50.4 %all-gather.11.cloned.1.call-done = bf16[1,1,1,1920,768]{4,3,2,1,0:T(8,128)(2,1)} async-done(((bf16[1,1,1,240,768]{4,3,2,1,0:T(8,128)(2,1)}), bf16[1,1,1,1920,768]{4,3,2,1,0:T(8,128)(2,1)}) %all-gather.11.cloned.1.call-update) | async-done | bytes 2949136 | tf_op jit(solution)/shard_map/all_gather | solution.py:228
  146.0 2.8 fusion.89
  150.1 2.5 all-gather.5
  153.6 2.7 fusion.27
  159.7 1.8 copy-done.1
  162.7 3.0 fusion.88
  165.8 20.1 %all-gather.4 = bf16[1,1,6,768]{2,1,0,3:T(2,128)(2,1)S(1)} all-gather(bf16[1,1,6,48]{2,1,0,3:T(2,128)(2,1)S(1)} %copy.269), channel_id=6, replica_groups=mesh['group'=2,'dp'=8,'tensor'=2] {'dp','tensor'}, dimensions={3}, use_global_device_ids=true | all-gather | bytes 9792 | tf_op jit(solution)/shard_map/all_gather | solution.py:215
  190.1 2.5 all_gather.46
  195.8 3.1 fusion.30
  198.9 2.6 all_gather.44
  201.5 3.5 convolution_add_fusion.3
  205.1 1.8 copy-done.103
  206.8 3.1 fusion.31
  211.3 7.1 reduce-scatter.19.cloned.1.call-done
  218.4 2.0 fusion.113
  222.4 2.5 fusion.103
  225.8 2.4 all_gather.47
  228.1 3.2 convert_reduce_fusion.1
  232.5 2.6 fusion.34
  235.2 2.4 all_gather.49
  237.5 5.3 convert_reduce_fusion
  244.0 2.6 fusion.32
  248.2 5.9 convolution_bitcast_fusion.1
  254.1 3.9 convolution_bitcast_fusion
  258.0 3.6 multiply_reduce_fusion.3
  261.6 3.3 fusion.108
  264.9 2.4 all_gather.48
  271.5 3.9 multiply_reduce_fusion.1
  276.4 2.5 all_gather.50
  283.1 4.0 multiply_reduce_fusion
  287.5 4.6 multiply_convert_fusion.1
  293.9 4.6 multiply_convert_fusion
  301.7 7.4 maximum_add_fusion.1
  309.4 5.4 convolution_bitcast_fusion.2
  314.8 3.6 convolution_bitcast_fusion.4
  320.2 2.9 convolution_bitcast_fusion.5
  323.1 5.2 copy.281
  331.7 6.2 maximum_add_fusion
  339.4 2.0 copy.316
  343.2 4.2 fusion.52
  347.5 3.9 fusion.50
  353.7 13.3 %reduce-scatter.37.cloned.1.call-done = f32[288,1]{1,0:T(8,128)} async-done(((f32[2304,1]{1,0:T(8,128)}), f32[288,1]{1,0:T(8,128)}) %reduce-scatter.37.cloned.1.call-update) | async-done | bytes 1168
  368.0 113.8 %reduce-scatter.35.cloned.1.call-done = f32[1,240,768]{2,1,0:T(8,128)} async-done(((f32[1,1920,768]{2,1,0:T(8,128)}), f32[1,240,768]{2,1,0:T(8,128)}) %reduce-scatter.35.cloned.1.call-update) | async-done | bytes 737296 | tf_op jit(solution)/shard_map/reduce_scatter | solution.py:409
  481.9 3.5 bitcast_subtract_fusion.1
  485.5 147.1 %reduce-scatter.33.cloned.1.call-done = f32[1,96,2688]{2,1,0:T(8,128)} async-done(((f32[1,768,2688]{2,1,0:T(8,128)}), f32[1,96,2688]{2,1,0:T(8,128)}) %reduce-scatter.33.cloned.1.call-update) | async-done | bytes 1032208 | tf_op jit(solution)/shard_map/reduce_scatter | solution.py:408
  632.6 4.3 bitcast_subtract_fusion
  637.6 53.5 %reduce-scatter.39.cloned.1.call-done = f32[48,6]{1,0:T(8,128)} async-done(((f32[768,6]{1,0:T(8,128)}), f32[48,6]{1,0:T(8,128)}) %reduce-scatter.39.cloned.1.call-update) | async-done | bytes 1168
  692.2 5.0 all-reduce.1
  699.0 2.6 reduce-scatter.27.cloned.1.call-done
  702.8 11.7 %reduce-scatter.31.cloned.1.call-done = f32[256,768]{1,0:T(8,128)} async-done(((f32[512,768]{1,0:T(8,128)}), f32[256,768]{1,0:T(8,128)}) %reduce-scatter.31.cloned.1.call-update) | async-done | bytes 786448 | tf_op jit(solution)/shard_map/reduce_scatter | solution.py:51
  717.1 2.0 copy.296
  719.1 2.0 copy.298
  721.1 2.0 copy.297
  723.1 52.1 %all-reduce.5.cloned.1.call-done = (f32[1,96,1,2688]{3,1,2,0:T(8,128)}, f32[1,1,240,768]{3,2,1,0:T(8,128)}) async-done(((f32[1,96,1,2688]{3,1,2,0:T(8,128)}, f32[1,1,240,768]{3,2,1,0:T(8,128)}), (f32[1,96,1,2688]{3,1,2,0:T(8,128)}, f32[1,1,240,768]{3,2,1,0:T(8,128)})) %all-reduce.5.cloned.1.call-update) | async-done | bytes 1769488 | tf_op jit(solution)/shard_map/psum | solution.py:430
  775.2 1.9 multiply_subtract_fusion
  777.1 2.0 copy.301
  779.1 2.0 copy.300
  781.2 2.0 copy.299
  (382 shorter events, 65.8 us)
Async XLA Ops:
  7.2 5.5 copy-start.89
  7.2 29.6 %copy-start.96 = (s32[2,1,2]{2,1,0:T(1,128)S(1)}, s32[2,1,2]{2,1,0:T(1,128)}, u32[]{:S(2)}) copy-start(s32[2,1,2]{2,1,0:T(1,128)} %param.29) | copy-start | bytes 52
  7.2 29.7 %copy-start.69 = (s32[2,1,8,6,3]{2,1,4,3,0:T(1,128)S(1)}, s32[2,1,8,6,3]{2,1,4,3,0:T(1,128)}, u32[]{:S(2)}) copy-start(s32[2,1,8,6,3]{2,1,4,3,0:T(1,128)} %param.30) | copy-start | bytes 3460
  7.2 30.3 %copy-start.92 = (s32[2,1]{0,1:T(1,128)S(1)}, s32[2,1]{0,1:T(1,128)}, u32[]{:S(2)}) copy-start(s32[2,1]{0,1:T(1,128)} %param.28) | copy-start | bytes 28
  7.3 31.6 %copy-start.29 = (bf16[2,1,256,768]{3,2,1,0:T(8,128)(2,1)S(1)}, bf16[2,1,256,768]{3,2,1,0:T(8,128)(2,1)}, u32[]{:S(2)}) copy-start(bf16[2,1,256,768]{3,2,1,0:T(8,128)(2,1)} %param.26) | copy-start | bytes 2359300
  7.3 79.3 %all-gather.9.cloned.1.call-start = ((), (), s32[]{:S(2)}) async-start(), calls=%async_computation.22 | async-start | bytes 4644864 | tf_op jit(solution)/shard_map/all_gather | solution.py:225
  9.5 136.6 %all-gather.11.cloned.1.call-start = ((), (), s32[]{:S(2)}) async-start(), calls=%async_computation.23 | async-start | bytes 3317760 | tf_op jit(solution)/shard_map/all_gather | solution.py:228
  11.4 176.2 %reduce-scatter.17.cloned.1.call-start = ((), (), s32[]{:S(2)}) async-start(), calls=%async_computation.12 | async-start | bytes 2359296 | tf_op jit(solution)/shard_map/reduce_scatter | solution.py:43
  41.2 45.4 %copy-start.54 = (bf16[1,1,512,768]{3,2,1,0:T(8,128)(2,1)}, bf16[1,1,512,768]{3,2,1,0:T(8,128)(2,1)S(1)}, u32[]{:S(2)}) copy-start(bf16[1,1,512,768]{3,2,1,0:T(8,128)(2,1)S(1)} %all-gather) | copy-start | bytes 2359300
  95.6 60.7 %copy-start.39 = (bf16[6,64,512]{2,1,0:T(8,128)(2,1)}, bf16[6,64,512]{2,1,0:T(8,128)(2,1)S(1)}, u32[]{:S(2)}) copy-start(bf16[6,64,512]{2,1,0:T(8,128)(2,1)S(1)} %fusion.49) | copy-start | bytes 1179652
  148.9 38.8 %reduce-scatter.21.cloned.1.call-start = ((), (), s32[]{:S(2)}) async-start(), calls=%async_computation.14 | async-start | bytes 2359296 | tf_op jit(solution)/shard_map/reduce_scatter | solution.py:43
  162.7 24.9 %copy-start.41 = (bf16[6,64,512]{2,1,0:T(8,128)(2,1)}, bf16[6,64,512]{2,1,0:T(8,128)(2,1)S(1)}, u32[]{:S(2)}) copy-start(bf16[6,64,512]{2,1,0:T(8,128)(2,1)S(1)} %fusion.48) | copy-start | bytes 1179652
  165.7 45.7 %reduce-scatter.23.cloned.1.call-start = ((), (), s32[]{:S(2)}) async-start(), calls=%async_computation.15 | async-start | bytes 2359296 | tf_op jit(solution)/shard_map/reduce_scatter | solution.py:43
  189.3 29.1 %copy-start.4 = (f32[256,768]{1,0:T(8,128)}, f32[256,768]{1,0:T(8,128)S(1)}, u32[]{:S(2)}) copy-start(f32[256,768]{1,0:T(8,128)S(1)} %get-tuple-element.358) | copy-start | bytes 2359300
  198.9 19.5 %reduce-scatter.19.cloned.1.call-start = ((), (), s32[]{:S(2)}) async-start(), calls=%async_computation.13 | async-start | bytes 2359296 | tf_op jit(solution)/shard_map/reduce_scatter | solution.py:43
  201.5 5.3 copy-start.61
  209.9 48.0 %reduce-scatter.25.cloned.1.call-start = ((), (), s32[]{:S(2)}) async-start(), calls=%async_computation.16 | async-start | bytes 2359296 | tf_op jit(solution)/shard_map/reduce_scatter | solution.py:51
  222.4 5.8 copy-start.62
  222.4 5.8 copy-start.104
  224.8 10.3 %copy-start.9 = (f32[256,768]{1,0:T(8,128)}, f32[256,768]{1,0:T(8,128)S(1)}, u32[]{:S(2)}) copy-start(f32[256,768]{1,0:T(8,128)S(1)} %get-tuple-element.334) | copy-start | bytes 2359300
  235.0 26.5 %reduce-scatter.29.cloned.1.call-start = ((), (), s32[]{:S(2)}) async-start(), calls=%async_computation.18 | async-start | bytes 2359296 | tf_op jit(solution)/shard_map/reduce_scatter | solution.py:51
  237.5 6.4 copy-start.99
  246.5 120.5 %reduce-scatter.37.cloned.1.call-start = ((), (), s32[]{:S(2)}) async-start(), calls=%async_computation.24 | async-start | bytes 1327104
  248.2 5.9 copy-start.102
  258.0 12.4 %slice-start = ((s8[6291456]{0:T(1024)(128)(4,1)}), s8[2097152]{0:T(1024)(128)(4,1)S(1)}, s32[]{:S(2)}) async-start(s8[6291456]{0:T(1024)(128)(4,1)} %bitcast.272), calls=%async_computation.27 | async-start | bytes 4194304
  261.6 5.7 copy-start.40
  261.6 8.8 %slice-start.1 = ((s8[6291456]{0:T(1024)(128)(4,1)}), s8[4194304]{0:T(1024)(128)(4,1)S(1)}, s32[]{:S(2)}) async-start(s8[6291456]{0:T(1024)(128)(4,1)} %bitcast.272), calls=%async_computation.28 | async-start | bytes 8388608
  264.9 5.5 copy-start.10
  270.4 11.6 %slice-start.2 = ((s8[6291456]{0:T(1024)(128)(4,1)}), s8[4194304]{0:T(1024)(128)(4,1)S(1)}, s32[]{:S(2)}) async-start(s8[6291456]{0:T(1024)(128)(4,1)} %bitcast.274), calls=%async_computation.29 | async-start | bytes 8388608
  271.5 15.8 %copy-start.43 = (bf16[6,64,512]{2,1,0:T(8,128)(2,1)}, bf16[6,64,512]{2,1,0:T(8,128)(2,1)S(1)}, u32[]{:S(2)}) copy-start(bf16[6,64,512]{2,1,0:T(8,128)(2,1)S(1)} %fusion.42) | copy-start | bytes 1179652
  271.5 10.5 %slice-start.3 = ((s8[6291456]{0:T(1024)(128)(4,1)}), s8[2097152]{0:T(1024)(128)(4,1)S(1)}, s32[]{:S(2)}) async-start(s8[6291456]{0:T(1024)(128)(4,1)} %bitcast.274), calls=%async_computation.30 | async-start | bytes 4194304
  276.3 5.7 copy-start.7
  292.1 6.4 copy-start.2
  301.7 180.2 %reduce-scatter.35.cloned.1.call-start = ((), (), s32[]{:S(2)}) async-start(), calls=%async_computation.21 | async-start | bytes 6635520 | tf_op jit(solution)/shard_map/reduce_scatter | solution.py:409
  309.1 323.5 %reduce-scatter.33.cloned.1.call-start = ((), (), s32[]{:S(2)}) async-start(), calls=%async_computation.20 | async-start | bytes 9289728 | tf_op jit(solution)/shard_map/reduce_scatter | solution.py:408
  309.4 5.4 copy-start.25
  309.4 5.4 copy-start.37
  323.1 5.2 copy-start.18
  338.0 353.1 %reduce-scatter.39.cloned.1.call-start = ((), (), s32[]{:S(2)}) async-start(), calls=%async_computation.25 | async-start | bytes 417792
  343.1 358.5 %reduce-scatter.27.cloned.1.call-start = ((), (), s32[]{:S(2)}) async-start(), calls=%async_computation.17 | async-start | bytes 2359296 | tf_op jit(solution)/shard_map/reduce_scatter | solution.py:51
  347.4 367.2 %reduce-scatter.31.cloned.1.call-start = ((), (), s32[]{:S(2)}) async-start(), calls=%async_computation.19 | async-start | bytes 2359296 | tf_op jit(solution)/shard_map/reduce_scatter | solution.py:51
  351.4 130.5 %copy-start.30 = (f32[1,1,1,240,768]{4,3,2,1,0:T(8,128)S(1)}, f32[1,1,1,240,768]{4,3,2,1,0:T(8,128)}, u32[]{:S(2)}) copy-start(f32[1,1,1,240,768]{4,3,2,1,0:T(8,128)} %param.37) | copy-start | bytes 2211844
  351.4 423.8 %all-reduce.5.cloned.1.call-start = ((), (), s32[]{:S(2)}) async-start(), calls=%async_computation.26 | async-start | bytes 3538944 | tf_op jit(solution)/shard_map/psum | solution.py:430
  353.7 278.9 %copy-start.12 = (f32[1,1,96,1,2688]{4,3,2,1,0:T(1,128)S(1)}, f32[1,1,96,1,2688]{4,3,2,1,0:T(1,128)}, u32[]{:S(2)}) copy-start(f32[1,1,96,1,2688]{4,3,2,1,0:T(1,128)} %param.32) | copy-start | bytes 3096580
  368.0 268.9 %copy-start.87 = (f32[1,288]{1,0:T(1,128)}, f32[1,288]{1,0:T(1,128)S(1)}, u32[]{:S(2)}) copy-start(f32[1,288]{1,0:T(1,128)S(1)} %copy.315) | copy-start | bytes 3460
  485.4 151.6 %copy-start.88 = (f32[1,1,288]{2,1,0:T(1,128)S(1)}, f32[1,1,288]{2,1,0:T(1,128)}, u32[]{:S(2)}) copy-start(f32[1,1,288]{2,1,0:T(1,128)} %param.45) | copy-start | bytes 3460
  485.4 151.6 %copy-start.90 = (f32[1,1,1,288]{3,2,1,0:T(1,128)S(1)}, f32[1,1,1,288]{3,2,1,0:T(1,128)}, u32[]{:S(2)}) copy-start(f32[1,1,1,288]{3,2,1,0:T(1,128)} %param.42) | copy-start | bytes 3460
  485.4 151.6 %copy-start.94 = (f32[1,1,1,288]{3,2,1,0:T(1,128)S(1)}, f32[1,1,1,288]{3,2,1,0:T(1,128)}, u32[]{:S(2)}) copy-start(f32[1,1,1,288]{3,2,1,0:T(1,128)} %param.44) | copy-start | bytes 3460
  485.4 151.6 %copy-start.95 = (f32[1,1,1,288]{3,2,1,0:T(1,128)S(1)}, f32[1,1,1,288]{3,2,1,0:T(1,128)}, u32[]{:S(2)}) copy-start(f32[1,1,1,288]{3,2,1,0:T(1,128)} %param.43) | copy-start | bytes 3460
  485.4 206.7 %copy-start.82 = (f32[1,6,48]{2,0,1:T(1,128)S(1)}, f32[1,6,48]{2,0,1:T(1,128)}, u32[]{:S(2)}) copy-start(f32[1,6,48]{2,0,1:T(1,128)} %param.50) | copy-start | bytes 3460
  485.4 206.7 %copy-start.84 = (f32[1,1,6,48]{3,1,2,0:T(1,128)S(1)}, f32[1,1,6,48]{3,1,2,0:T(1,128)}, u32[]{:S(2)}) copy-start(f32[1,1,6,48]{3,1,2,0:T(1,128)} %param.47) | copy-start | bytes 3460
  485.4 206.7 %copy-start.85 = (f32[1,1,6,48]{3,1,2,0:T(1,128)S(1)}, f32[1,1,6,48]{3,1,2,0:T(1,128)}, u32[]{:S(2)}) copy-start(f32[1,1,6,48]{3,1,2,0:T(1,128)} %param.48) | copy-start | bytes 3460
  485.4 206.7 %copy-start.86 = (f32[1,1,6,48]{3,1,2,0:T(1,128)S(1)}, f32[1,1,6,48]{3,1,2,0:T(1,128)}, u32[]{:S(2)}) copy-start(f32[1,1,6,48]{3,1,2,0:T(1,128)} %param.49) | copy-start | bytes 3460
  485.4 211.8 %copy-start.93 = (f32[1,1,288]{2,1,0:T(1,128)S(1)}, f32[1,1,288]{2,1,0:T(1,128)}, u32[]{:S(2)}) copy-start(f32[1,1,288]{2,1,0:T(1,128)} %param.46) | copy-start | bytes 3460
  485.4 212.9 %copy-start.91 = (f32[1,6,48]{2,0,1:T(1,128)S(1)}, f32[1,6,48]{2,0,1:T(1,128)}, u32[]{:S(2)}) copy-start(f32[1,6,48]{2,0,1:T(1,128)} %param.51) | copy-start | bytes 3460
  485.5 216.1 %copy-start.11 = (f32[256,768]{1,0:T(8,128)S(1)}, f32[256,768]{1,0:T(8,128)}, u32[]{:S(2)}) copy-start(f32[256,768]{1,0:T(8,128)} %copy-done.10) | copy-start | bytes 2359300
  636.9 77.6 %copy-start.8 = (f32[256,768]{1,0:T(8,128)S(1)}, f32[256,768]{1,0:T(8,128)}, u32[]{:S(2)}) copy-start(f32[256,768]{1,0:T(8,128)} %copy-done.7) | copy-start | bytes 2359300
  692.1 24.9 %copy-start.66 = (f32[1,6,48]{2,0,1:T(1,128)}, f32[1,6,48]{2,0,1:T(1,128)S(1)}, u32[]{:S(2)}) copy-start(f32[1,6,48]{2,0,1:T(1,128)S(1)} %copy.317) | copy-start | bytes 3460
  702.8 14.2 %copy-start.13 = (f32[1,96,2688]{2,1,0:T(8,128)S(1)}, f32[1,96,2688]{2,1,0:T(8,128)}, u32[]{:S(2)}) copy-start(f32[1,96,2688]{2,1,0:T(8,128)} %reduce-scatter.33.cloned.1.call-done) | copy-start | bytes 3096580
  715.8 5.3 copy-start.14
  717.1 58.1 %copy-start.16 = (f32[1,96,1,2688]{3,2,1,0:T(1,128)S(1)}, f32[1,96,1,2688]{3,2,1,0:T(1,128)}, u32[]{:S(2)}) copy-start(f32[1,96,1,2688]{3,2,1,0:T(1,128)} %param.35) | copy-start | bytes 3096580
  777.1 6.1 copy-start.31
  777.1 6.1 copy-start.58
  777.1 6.1 copy-start.59
  (60 other events, 130.4 us)
Sparse Core Ops, SparseCore 0:
  10.9 75.6 all-gather.8
  89.4 56.6 all-gather.10
  149.0 7.6 reduce-scatter.16
  165.8 8.0 reduce-scatter.20
  199.0 6.3 reduce-scatter.22
  210.1 8.2 reduce-scatter.18
  235.2 10.2 reduce-scatter.24
  248.4 10.2 reduce-scatter.28
  301.8 65.2 reduce-scatter.36
  371.1 110.7 reduce-scatter.34
  485.6 146.9 reduce-scatter.32
  636.5 54.5 reduce-scatter.38
  693.5 8.0 reduce-scatter.26
  704.3 10.2 reduce-scatter.30
  718.0 57.1 all-reduce.4
where the time goes:
time: 799 us; the launch traced here: 792 us
  waiting for transfers between devices  497 us (62%)
  matrix products  92.2 us (12%)
  blocking collectives  68.5 us (9%)
  other arithmetic  66.5 us (8%)
  local copies, waits for them, and re-layouts  48.2 us (6%)
  between operations  17.4 us (2%)
    reduce_scatter x1, waiting for transfers between devices, on_device(): lax.psum_scatter(merged[0], 'dp', scatter_dimension=1, tiled=True)  147 us
    reduce_scatter x1, waiting for transfers between devices, on_device(): lax.psum_scatter(merged[1], 'dp', scatter_dimension=1, tiled=True)  114 us
    unnamed x17, waiting for transfers between devices  67.1 us
    psum x1, waiting for transfers between devices, on_device(): diff_sums = lax.psum((diffs[0], diffs[1], diffs[2], diffs[3]), 'group')  52.1 us
    all_gather x1, waiting for transfers between devices, on_device(): lax.all_gather(narrow_inner[0, 0, 0].astype(jnp.bfloat16), 'dp', axis=0,...  50.4 us
    all_gather x1, waiting for transfers between devices, on_device(): lax.all_gather(wide_inner[0, 0, :, 0, :].astype(jnp.bfloat16), 'dp', axis...  45.3 us
    unnamed x245, local copies, waits for them, and re-layouts  37.6 us
    unnamed x1, blocking collectives  23.8 us
  transfers between devices with their start and end apart: 15, of which 10 were waited for; matrix products, arithmetic and copies ran while one was open for 16% of the time, Pallas kernels for 0%

commit v1 on v0

--- a/solution.py
+++ b/solution.py
@@ -1,6 +1,8 @@
 import jax
 import jax.numpy as jnp
 from jax import lax
+from jax.experimental import pallas as pl
+from jax.experimental.pallas import tpu as pltpu
 from jax.sharding import PartitionSpec as P
 
 BETA_ONE = 0.9
@@ -12,6 +14,320 @@
 OUTER_RATE = 0.7
 NORM_EPS = 1e-06
 MASKED = -1e30
+
+MESH = pl.DeviceIdType.MESH
+ZS = 4
+F32, BF16 = jnp.float32, jnp.bfloat16
+
+
+def place():
+    d = lax.axis_index("dp")
+    return d // 2, lax.rem(d, 2)
+
+
+def neighbours():
+    g, t = lax.axis_index("group"), lax.axis_index("tensor")
+    z, x = place()
+    return dict(
+        x=(g, z * 2 + (1 - x), t),
+        up=(g, (z + 1) * 2 + x, t),
+        down=(g, (z - 1) * 2 + x, t),
+        core=(g, z * 2 + x, 1 - t),
+        group=(1 - g, z * 2 + x, t),
+    )
+
+
+def entry_barrier():
+    z, _ = place()
+    near = neighbours()
+    bar = pltpu.get_barrier_semaphore()
+
+    def greet(name):
+        pl.semaphore_signal(bar, inc=1, device_id=near[name], device_id_type=MESH)
+
+    for name in ("x", "core", "group"):
+        greet(name)
+    pl.when(z < ZS - 1)(lambda: greet("up"))
+    pl.when(z > 0)(lambda: greet("down"))
+    pl.semaphore_wait(bar, 3 + (z + 2) // 3 + (ZS + 1 - z) // 3)
+
+
+WAYS = {"x": 0, "up": 1, "down": 2}
+
+
+class Gather:
+    def __init__(self, view, ssem, rsem):
+        self.view, self.ssem, self.rsem = view, ssem, rsem
+        self.near = neighbours()
+        self.z, self.x = place()
+
+    def copy(self, g, zsrc, xsrc, way):
+        ref = self.view(g, zsrc * 2 + xsrc)
+        return pltpu.make_async_remote_copy(
+            src_ref=ref,
+            dst_ref=ref,
+            send_sem=self.ssem.at[g, zsrc, WAYS[way]],
+            recv_sem=self.rsem.at[g, zsrc * 2 + xsrc],
+            device_id=self.near[way],
+            device_id_type=MESH,
+        )
+
+    def own(self, g, only=None):
+        z, x = self.z, self.x
+        ok = (z >= 0) if only is None else only(z)
+        pl.when(ok)(lambda: self.copy(g, z, x, "x").start())
+        pl.when(ok & (z < ZS - 1))(lambda: self.copy(g, z, x, "up").start())
+        pl.when(ok & (z > 0))(lambda: self.copy(g, z, x, "down").start())
+
+    def relay(self, g, k, only=None):
+        z, x = self.z, self.x
+        for way, src in (("up", z - k), ("down", z + k)):
+            ok = (src >= 0) if way == "up" else (src < ZS)
+            if only is not None:
+                ok = ok & only(src)
+            more = (z < ZS - 1) if way == "up" else (z > 0)
+
+            @pl.when(ok)
+            def _():
+                self.copy(g, src, x, way).wait_recv()
+                self.copy(g, src, x, "x").start()
+                pl.when(more)(lambda: self.copy(g, src, x, way).start())
+
+    def across(self, g, srcs=range(ZS)):
+        for zsrc in srcs:
+            self.copy(g, zsrc, 1 - self.x, "x").wait_recv()
+
+    def drain(self, g, srcs=range(ZS)):
+        z, x = self.z, self.x
+        for zsrc in srcs:
+            self.copy(g, zsrc, x, "x").wait_send()
+            pl.when((zsrc <= z) & (z < ZS - 1))(lambda: self.copy(g, zsrc, x, "up").wait_send())
+            pl.when((zsrc >= z) & (z > 0))(lambda: self.copy(g, zsrc, x, "down").wait_send())
+
+
+def far_order(z, k):
+    if k == 0:
+        return 3 * (1 - z // 2)
+    if k == 1:
+        return lax.rem(2 + 3 * z, 5)
+    if k == 2:
+        return 1 + lax.rem(z, 2)
+    return z
+
+
+class Scatter:
+    def __init__(self, source, xbuf, zbuf, xs, xr, zs, zr):
+        self.source, self.xbuf, self.zbuf = source, xbuf, zbuf
+        self.xs, self.xr, self.zs, self.zr = xs, xr, zs, zr
+        self.near = neighbours()
+        self.z, self.x = place()
+
+    def xcopy(self, g, row):
+        return pltpu.make_async_remote_copy(
+            src_ref=self.source(g, row * 2 + (1 - self.x)),
+            dst_ref=self.xbuf(g, row),
+            send_sem=self.xs.at[g, row],
+            recv_sem=self.xr.at[g, row],
+            device_id=self.near["x"],
+            device_id_type=MESH,
+        )
+
+    def zcopy(self, g, row, slot, way):
+        return pltpu.make_async_remote_copy(
+            src_ref=self.xbuf(g, row),
+            dst_ref=self.zbuf(g, slot),
+            send_sem=self.zs.at[g, row],
+            recv_sem=self.zr.at[g, slot],
+            device_id=self.near[way],
+            device_id_type=MESH,
+        )
+
+    def send(self, g, k, only=None):
+        row = far_order(self.z, k)
+        ok = (row >= 0) if only is None else only(row)
+        pl.when(ok)(lambda: self.xcopy(g, row).start())
+
+    def pass_on(self, g, k, only=None):
+        z, x = self.z, self.x
+        row = far_order(z, k)
+        ok = (row >= 0) if only is None else only(row)
+
+        @pl.when(ok)
+        def _():
+            self.xcopy(g, row).wait_recv()
+            below = z < row
+            further = (below & (z > 0)) | ((z > row) & (z < ZS - 1))
+            src, buf = self.source(g, row * 2 + x), self.xbuf(g, row)
+
+            @pl.when(further)
+            def _():
+                self.zcopy(g, row, row, "up").wait_recv()
+                buf[...] = (
+                    src[...].astype(F32) + buf[...].astype(F32) + self.zbuf(g, row)[...].astype(F32)
+                ).astype(BF16)
+
+            @pl.when(jnp.logical_not(further))
+            def _():
+                buf[...] = (src[...].astype(F32) + buf[...].astype(F32)).astype(BF16)
+
+            pl.when(below & (z + 1 < row))(lambda: self.zcopy(g, row, row, "up").start())
+            pl.when(below & (z + 1 == row))(lambda: self.zcopy(g, row, ZS, "up").start())
+            pl.when(z > row)(lambda: self.zcopy(g, row, row, "down").start())
+
+    def finish(self, g, result, only=None):
+        z, x = self.z, self.x
+        ok = (z >= 0) if only is None else only(z)
+
+        @pl.when(ok)
+        def _():
+            self.xcopy(g, z).wait_recv()
+            out = result(g)
+            out[...] = self.source(g, z * 2 + x)[...].astype(F32) + self.xbuf(g, z)[...].astype(F32)
+
+            @pl.when(z < ZS - 1)
+            def _():
+                self.zcopy(g, z, z, "down").wait_recv()
+                out[...] += self.zbuf(g, z)[...].astype(F32)
+
+            @pl.when(z > 0)
+            def _():
+                self.zcopy(g, z, ZS, "up").wait_recv()
+                out[...] += self.zbuf(g, ZS)[...].astype(F32)
+
+    def drain(self, g, k, only=None):
+        row = far_order(self.z, k)
+        ok = (row >= 0) if only is None else only(row)
+
+        @pl.when(ok)
+        def _():
+            self.xcopy(g, row).wait_send()
+            if k < 3:
+                self.zcopy(g, row, row, "up").wait_send()
+
+
+VMEM_SPEC = pl.BlockSpec(memory_space=pltpu.VMEM)
+DMA = pltpu.SemaphoreType.DMA
+BIG_VMEM = 56 * 1024 * 1024
+
+
+def first_row(row):
+    return row == 0
+
+
+def other_rows(row):
+    return row > 0
+
+
+def shard_view(wide, narrow, split):
+    rows, cols = wide.shape[0] // 8, wide.shape[1]
+    deep = narrow.shape[0] // 8
+
+    def view(g, shard):
+        if g == 2:
+            return narrow.at[pl.ds(pl.multiple_of(shard * deep, deep), deep)]
+        at = pl.ds(pl.multiple_of(shard * rows, rows), rows)
+        return wide.at[at, pl.ds(0, split)] if g == 0 else wide.at[at, pl.ds(split, cols - split)]
+
+    return view
+
+
+def gather_kernel(split, wide_own, narrow_own, wide, narrow, ssem, rsem):
+    z, x = place()
+    shard = z * 2 + x
+    rows, deep = wide_own.shape[0], narrow_own.shape[0]
+    wide[pl.ds(pl.multiple_of(shard * rows, rows), rows), :] = wide_own[...].astype(BF16)
+    narrow[pl.ds(pl.multiple_of(shard * deep, deep), deep), :] = narrow_own[...].astype(BF16)
+    entry_barrier()
+    work = Gather(shard_view(wide, narrow, split), ssem, rsem)
+    order = (0, 2, 1)
+    work.own(0)
+    for at, g in enumerate(order):
+        work.relay(g, 1)
+        if at < 2:
+            work.own(order[at + 1])
+        work.relay(g, 2)
+        work.relay(g, 3)
+    for g in range(3):
+        work.across(g)
+    for g in range(3):
+        work.drain(g)
+
+
+def gather_weights(wide_own, narrow_own, split):
+    return pl.pallas_call(
+        lambda *refs: gather_kernel(split, *refs),
+        out_shape=(
+            jax.ShapeDtypeStruct((8 * wide_own.shape[0], wide_own.shape[1]), BF16),
+            jax.ShapeDtypeStruct((8 * narrow_own.shape[0], narrow_own.shape[1]), BF16),
+        ),
+        in_specs=[VMEM_SPEC] * 2,
+        out_specs=(VMEM_SPEC,) * 2,
+        scratch_shapes=[DMA((3, 4, 3)), DMA((3, 8))],
+        compiler_params=pltpu.CompilerParams(
+            collective_id=1, has_side_effects=True, vmem_limit_bytes=BIG_VMEM
+        ),
+        name="gather_weights",
+    )(wide_own, narrow_own)
+
+
+def scatter_kernel(split, wide, narrow, wide_out, narrow_out, xw, xn, zw, zn, xs, xr, zs, zr):
+    entry_barrier()
+    cols = wide.shape[1]
+
+    def half(g):
+        return pl.ds(0, split) if g == 0 else pl.ds(split, cols - split)
+
+    work = Scatter(
+        shard_view(wide, narrow, split),
+        lambda g, row: xn.at[row] if g == 2 else xw.at[row, :, half(g)],
+        lambda g, row: zn.at[row] if g == 2 else zw.at[row, :, half(g)],
+        xs,
+        xr,
+        zs,
+        zr,
+    )
+
+    def result(g):
+        return narrow_out if g == 2 else wide_out.at[:, half(g)]
+
+    for g in (2, 1, 0):
+        for k in range(4):
+            work.send(g, k)
+    for g in (2, 1, 0):
+        for k in range(3):
+            work.pass_on(g, k)
+        work.finish(g, result)
+    for g in (2, 1, 0):
+        for k in range(4):
+            work.drain(g, k)
+
+
+def scatter_grads(wide, narrow, split):
+    rows, cols = wide.shape[0] // 8, wide.shape[1]
+    deep, width = narrow.shape[0] // 8, narrow.shape[1]
+    return pl.pallas_call(
+        lambda *refs: scatter_kernel(split, *refs),
+        out_shape=(
+            jax.ShapeDtypeStruct((rows, cols), F32),
+            jax.ShapeDtypeStruct((deep, width), F32),
+        ),
+        in_specs=[VMEM_SPEC] * 2,
+        out_specs=(VMEM_SPEC,) * 2,
+        scratch_shapes=[
+            pltpu.VMEM((ZS, rows, cols), BF16),
+            pltpu.VMEM((ZS, deep, width), BF16),
+            pltpu.VMEM((ZS + 1, rows, cols), BF16),
+            pltpu.VMEM((ZS + 1, deep, width), BF16),
+            DMA((3, ZS)),
+            DMA((3, ZS)),
+            DMA((3, ZS)),
+            DMA((3, ZS + 1)),
+        ],
+        compiler_params=pltpu.CompilerParams(
+            collective_id=2, has_side_effects=True, vmem_limit_bytes=BIG_VMEM
+        ),
+        name="scatter_grads",
+    )(wide, narrow)
 
 
 def gelu_tanh(values):
@@ -215,22 +531,31 @@
     norms_full = lax.all_gather(
         norms_inner[0].astype(jnp.bfloat16), ("dp", "tensor"), axis=2, tiled=True
     ).astype(jnp.float32)
+    fast = lax.axis_size("dp") == 8 and wide_inner.shape[2] % 16 == 0 and layers == 1
+    if fast:
+        gathered = (
+            *gather_weights(wide_inner[0, 0, :, 0, :], narrow_inner[0, 0, 0], 3 * attn_cols),
+            lax.all_gather(bias_inner[0, 0, 0].astype(jnp.bfloat16), "dp", axis=0, tiled=True),
+        )
     outs_rows = []
     grads_rows = []
     collected = []
     collected_rows = []
     for micro_index in range(micro_count):
-        weights = [
-            (
-                lax.all_gather(
-                    wide_inner[0, 0, :, 0, :].astype(jnp.bfloat16), "dp", axis=0, tiled=True
-                ),
-                lax.all_gather(
-                    narrow_inner[0, 0, 0].astype(jnp.bfloat16), "dp", axis=0, tiled=True
-                ),
-                lax.all_gather(bias_inner[0, 0, 0].astype(jnp.bfloat16), "dp", axis=0, tiled=True),
-            )
-        ]
+        if fast:
+            weights = [gathered]
+        else:
+            weights = [
+                (
+                    lax.all_gather(
+                        wide_inner[0, 0, :, 0, :].astype(jnp.bfloat16), "dp", axis=0, tiled=True
+                    ),
+                    lax.all_gather(
+                        narrow_inner[0, 0, 0].astype(jnp.bfloat16), "dp", axis=0, tiled=True
+                    ),
+                    lax.all_gather(bias_inner[0, 0, 0].astype(jnp.bfloat16), "dp", axis=0, tiled=True),
+                )
+            ]
         length = lengths[micro_index, 0]
         key_ok = jnp.arange(seq_len, dtype=jnp.int32) < length
         row_ok = (own_rows < length).astype(jnp.float32)[:, None]
@@ -404,11 +729,17 @@
     merged_rows = collected_rows[0]
     for extra in collected_rows[1:]:
         merged_rows = merged_rows + extra
-    shards = (
-        lax.psum_scatter(merged[0], "dp", scatter_dimension=1, tiled=True),
-        lax.psum_scatter(merged[1], "dp", scatter_dimension=1, tiled=True),
-        lax.psum_scatter(merged[2], "dp", scatter_dimension=1, tiled=True),
-    )
+    if fast:
+        wide_sum, narrow_sum = scatter_grads(
+            merged[0][0].astype(BF16), merged[1][0].astype(BF16), 3 * attn_cols
+        )
+        shards = (wide_sum[None], narrow_sum[None])
+    else:
+        shards = (
+            lax.psum_scatter(merged[0], "dp", scatter_dimension=1, tiled=True),
+            lax.psum_scatter(merged[1], "dp", scatter_dimension=1, tiled=True),
+        )
+    shards = shards + (lax.psum_scatter(merged[2], "dp", scatter_dimension=1, tiled=True),)
     row_shard = lax.psum_scatter(merged_rows, ("dp", "tensor"), scatter_dimension=2, tiled=True)
     grads = (
         shards[0][None, :, :, None, :],
@@ -427,8 +758,15 @@
         for kind in range(4)
     ]
     diffs = tuple((anchors[kind] - updated[kind][0][0] for kind in range(4)))
-    diff_sums = lax.psum((diffs[0], diffs[1], diffs[2], diffs[3]), "group")
     group_count = lax.axis_size("group")
+    if fast and group_count == 2:
+        sent = tuple(diff.astype(BF16) for diff in diffs)
+        diff_sums = tuple(
+            here.astype(F32) + lax.ppermute(here, "group", ((0, 1), (1, 0))).astype(F32)
+            for here in sent
+        )
+    else:
+        diff_sums = lax.psum((diffs[0], diffs[1], diffs[2], diffs[3]), "group")
     results = []
     for kind in range(4):
         mean_diff = diff_sums[kind] / group_count

time: 799 us -> 480 us (0.60)
  waiting for transfers between devices: 497 us -> 11.8 us
  Pallas kernels: 0 us -> 179 us
  other arithmetic: 66.5 us -> 56.4 us
    reduce_scatter x2 -> x0, waiting for transfers between devices: 261 us -> none  [the longest x1 147 us: on_device(): lax.psum_scatter(merged[0], 'dp', scatter_dimension=1, tiled=True)]
    pallas_call x0 -> x2, Pallas kernels: none -> 179 us  [the longest x1 95 us: scatter_grads(): pl.pallas_call(lambda *refs: scatter_kernel(split, *refs), out_shape=(jax...]
    all_gather x2 -> x0, waiting for transfers between devices: 95.8 us -> none  [the longest x1 50.4 us: on_device(): lax.all_gather(narrow_inner[0, 0, 0].astype(jnp.bfloat16), 'dp', axis=0,...]
    unnamed x17 -> x12, waiting for transfers between devices: 67.1 us -> 0.19 us
    psum x1 -> x0, waiting for transfers between devices: 52.1 us -> none  [on_device(): diff_sums = lax.psum((diffs[0], diffs[1], diffs[2], diffs[3]), 'group')]
    reduce_scatter x4, waiting for transfers between devices: 14.4 us -> 0.04 us  [sum_backward(): return lax.psum_scatter(values, 'tensor', scatter_dimension=0, tiled=True)]
    add x3 -> x1, other arithmetic: 13.6 us -> 0.02 us  [on_device(): merged = jax.tree.map(jnp.add, merged, extra)]
    convert_element_type x1 -> x6, other arithmetic: 1.89 us -> 15.1 us  [the longest x4 7.04 us: on_device(): sent = tuple((diff.astype(BF16) for diff in diffs))]
  transfers between devices with their start and end apart: 15 -> 14, of which waited for: 10 -> 2; matrix products, arithmetic and copies ran while one was open for 16% -> 22% of each run, Pallas kernels for 0% -> 20%
where the time goes in v1:
time: 480 us; the launch traced here: 473 us
  Pallas kernels  179 us (37%)
  matrix products  86.4 us (18%)
  blocking collectives  64.7 us (13%)
  other arithmetic  56.4 us (12%)
  local copies, waits for them, and re-layouts  51.4 us (11%)
  between operations  17.6 us (4%)
  waiting for transfers between devices  11.8 us (2%)
  starting transfers between devices  5.11 us (1%)
    pallas_call x1, Pallas kernels, scatter_grads(): pl.pallas_call(lambda *refs: scatter_kernel(split, *refs), out_shape=(jax...  95 us
    pallas_call x1, Pallas kernels, gather_weights(): pl.pallas_call(lambda *refs: gather_kernel(split, *refs), out_shape=(jax....  84.5 us
    unnamed x228, local copies, waits for them, and re-layouts  42.9 us
    unnamed x1, blocking collectives  23.3 us
    all_gather x1, blocking collectives, on_device(): lax.all_gather(norms_inner[0].astype(jnp.bfloat16), ('dp', 'tensor'), axi...  21.5 us
    all_gather x4, blocking collectives, rows_forward(): return lax.all_gather(values, 'tensor', axis=0, tiled=True)  10.1 us
    all_gather x4, blocking collectives, rows_backward(): return lax.all_gather(values, 'tensor', axis=0, tiled=True)  9.78 us
  transfers between devices with their start and end apart: 14, of which 2 were waited for; matrix products, arithmetic and copies ran while one was open for 22% of the time, Pallas kernels for 20%

profile of v1, /device:TPU:0, one launch (start us, length us, event | category | flops | bytes accessed | tf_op | source)
XLA Modules:
  0.0 472.9 jit_solution(6077130725988153112)
XLA Ops:
  13.0 23.3 %all-reduce = bf16[2304]{0:T(1024)(128)(2,1)S(1)} all-reduce(bf16[2304]{0:T(1024)(128)(2,1)S(1)} %dynamic-update-slice), channel_id=3, replica_groups=mesh['group'=2,'dp'=8,'tensor'=2] {'dp'}, use_global_device_ids=true, to_apply=%add | all-reduce | flops 2304 | bytes 9216
  38.8 2.4 all-gather
  42.3 84.5 %gather_weights.1 = (bf16[768,2688]{1,0:T(8,128)(2,1)}, bf16[1920,768]{1,0:T(8,128)(2,1)}) custom-call(f32[96,2688]{1,0:T(8,128)} %bitcast.273, f32[240,768]{1,0:T(8,128)} %bitcast.282), custom_call_target="tpu_custom_call" | custom-call | tf_op jit(solution)/shard_map/gather_weights/pallas_call | solution.py:257
  126.8 2.6 fusion.31
  129.6 1.7 fusion.146
  132.2 1.8 copy-done.1
  136.0 2.8 fusion.107
  140.0 2.6 all-gather.3
  142.6 2.9 fusion.30
  145.7 1.7 fusion.147
  148.3 1.8 copy-done
  152.0 2.8 fusion.105
  155.0 21.5 %all-gather.2 = bf16[1,1,6,768]{2,1,0,3:T(2,128)(2,1)S(1)} all-gather(bf16[1,1,6,48]{2,1,0,3:T(2,128)(2,1)S(1)} %copy.193), channel_id=4, replica_groups=mesh['group'=2,'dp'=8,'tensor'=2] {'dp','tensor'}, dimensions={3}, use_global_device_ids=true | all-gather | bytes 9792 | tf_op jit(solution)/shard_map/all_gather | solution.py:531
  178.2 1.7 fusion.136
  180.7 2.5 all_gather.35
  184.7 1.7 copy-done.87
  186.3 3.1 fusion.36
  189.5 2.6 all_gather.33
  192.1 3.5 convolution_add_fusion.3
  195.7 1.6 copy-done.89
  197.4 3.1 fusion.38
  201.9 7.2 %reduce-scatter.17.cloned.1.call-done = f32[256,768]{1,0:T(8,128)} async-done(((f32[512,768]{1,0:T(8,128)}), f32[256,768]{1,0:T(8,128)}) %reduce-scatter.17.cloned.1.call-update) | async-done | bytes 786448 | tf_op jit(solution)/shard_map/reduce_scatter | solution.py:359
  209.1 2.0 fusion.135
  212.5 1.9 fusion.126
  215.3 2.5 all_gather.36
  217.8 3.2 convert_reduce_fusion.1
  222.2 2.6 fusion.46
  224.9 2.4 all_gather.38
  227.3 5.5 %convert_reduce_fusion = (f32[1536]{0:T(1024)S(1)}, bf16[512,1536]{1,0:T(8,128)(2,1)S(1)}) fusion(f32[512,1536]{1,0:T(8,128)} %copy-done.87, bf16[512,768]{1,0:T(8,128)(2,1)S(1)} %all_gather.38, bf16[1920,768]{1,0:T(8,128)(2,1)} %get-tuple-element.134), kind=kOutput, calls=%fused_computation.49 | convolution fusion | flops 1225259520 | bytes 7870464 | tf_op jit(solution)/shard_map/sd,fd->sf/dot_general | solution.py:652
  233.9 2.6 fusion.44
  239.0 5.1 %fusion.149 = f32[768,1536]{1,0:T(8,128)} fusion(bf16[512,768]{1,0:T(8,128)(2,1)S(1)} %copy-done.20, bf16[512,1536]{1,0:T(8,128)(2,1)} %copy-done.39), kind=kOutput, calls=%fused_computation.298 | convolution fusion | flops 1207959552 | bytes 7077888 | tf_op jit(solution)/shard_map/sd,sf->df/dot_general | solution.py:657
  244.1 3.6 fusion.148
  247.7 3.9 fusion.124
  251.6 4.0 fusion.125
  255.5 3.0 multiply_reduce_fusion.3
  258.6 2.7 fusion.131
  262.2 2.5 all_gather.37
  265.6 1.6 convolution_convert_fusion.1
  267.3 1.8 fusion.54
  270.6 1.8 multiply_convert_fusion.1
  273.1 1.8 fusion.51
  276.1 2.4 all_gather.39
  282.1 4.6 multiply_reduce_fusion
  288.3 2.3 copy.238
  290.8 6.4 %multiply_convert_fusion = bf16[6,512,512]{1,2,0:T(8,128)(2,1)S(1)} fusion(f32[6,512,512]{1,2,0:T(8,128)} %get-tuple-element.381, f32[6,512,512]{1,2,0:T(8,128)} %copy-done, f32[6,512]{1,0:T(8,128)} %get-tuple-element.380, f32[6,512]{1,0:T(8,128)S(1)} %log_add_fusion), kind=kLoop, calls=%fused_computation.2 | loop fusion | flops 6291456 | bytes 15753216 | tf_op jit(solution)/shard_map/while/body/eval_jaxpr/convert_element_type | solution.py:448
  300.7 3.5 bitcast_reduce_fusion
  304.3 4.3 fusion.64
  308.7 2.8 maximum_bitcast_fusion
  312.5 5.7 %fusion.1.refs_1_ = bf16[1920,768]{1,0:T(8,128)(2,1)} fusion(f32[1536,768]{1,0:T(8,128)} %fusion.124, f32[384,768]{1,0:T(8,128)S(1)} %fusion.150, f32[1536,768]{1,0:T(8,128)} %fusion.125, f32[384,768]{1,0:T(8,128)S(1)} %fusion.151), kind=kLoop, calls=%fused_computation.17 | loop fusion | flops 5898240 | bytes 14745600 | tf_op jit(solution)/shard_map/convert_element_type | solution.py:734
  322.3 2.4 fusion.refs_0_
  324.8 95.0 %scatter_grads.1 = (f32[96,2688]{1,0:T(8,128)}, f32[240,768]{1,0:T(8,128)}) custom-call(bf16[768,2688]{1,0:T(8,128)(2,1)} %fusion.refs_0_, bf16[1920,768]{1,0:T(8,128)(2,1)} %fusion.1.refs_1_), custom_call_target="tpu_custom_call" | custom-call | tf_op jit(solution)/shard_map/scatter_grads/pallas_call | solution.py:308
  419.7 3.2 copy.217
  423.0 2.8 fusion.100
  425.9 4.0 fusion.62
  431.6 1.9 collective-permute-start.2
  433.5 3.6 fusion.70
  437.2 2.0 copy.219
  439.2 2.0 copy.218
  442.9 2.1 collective-permute-start.3
  445.5 4.4 collective-permute-done.3
  450.5 2.8 multiply_subtract_fusion.1
  454.8 2.0 copy.222
  456.9 2.0 copy.221
  458.9 2.0 copy.220
  (353 shorter events, 57.4 us)
Async XLA Ops:
  7.2 33.9 %copy-start.9 = (f32[1,1,96,1,2688]{4,3,2,1,0:T(1,128)S(1)}, f32[1,1,96,1,2688]{4,3,2,1,0:T(1,128)}, u32[]{:S(2)}) copy-start(f32[1,1,96,1,2688]{4,3,2,1,0:T(1,128)} %param.32) | copy-start | bytes 3096580
  7.2 171.0 %reduce-scatter.15.cloned.1.call-start = ((), (), s32[]{:S(2)}) async-start(), calls=%async_computation.10 | async-start | bytes 2359296 | tf_op jit(solution)/shard_map/reduce_scatter | solution.py:359
  41.1 88.3 %copy-start.53 = (bf16[1,1,512,768]{3,2,1,0:T(8,128)(2,1)}, bf16[1,1,512,768]{3,2,1,0:T(8,128)(2,1)S(1)}, u32[]{:S(2)}) copy-start(bf16[1,1,512,768]{3,2,1,0:T(8,128)(2,1)S(1)} %all-gather) | copy-start | bytes 2359300
  138.8 39.4 %reduce-scatter.19.cloned.1.call-start = ((), (), s32[]{:S(2)}) async-start(), calls=%async_computation.12 | async-start | bytes 2359296 | tf_op jit(solution)/shard_map/reduce_scatter | solution.py:359
  154.8 23.4 %copy-start.24 = (bf16[2,1,256,768]{3,2,1,0:T(8,128)(2,1)S(1)}, bf16[2,1,256,768]{3,2,1,0:T(8,128)(2,1)}, u32[]{:S(2)}) copy-start(bf16[2,1,256,768]{3,2,1,0:T(8,128)(2,1)} %param.26) | copy-start | bytes 2359300
  154.8 47.0 %reduce-scatter.21.cloned.1.call-start = ((), (), s32[]{:S(2)}) async-start(), calls=%async_computation.13 | async-start | bytes 2359296 | tf_op jit(solution)/shard_map/reduce_scatter | solution.py:359
  179.9 29.2 %copy-start.2 = (f32[256,768]{1,0:T(8,128)}, f32[256,768]{1,0:T(8,128)S(1)}, u32[]{:S(2)}) copy-start(f32[256,768]{1,0:T(8,128)S(1)} %get-tuple-element.336) | copy-start | bytes 2359300
  189.5 19.6 %reduce-scatter.17.cloned.1.call-start = ((), (), s32[]{:S(2)}) async-start(), calls=%async_computation.11 | async-start | bytes 2359296 | tf_op jit(solution)/shard_map/reduce_scatter | solution.py:359
  192.1 5.2 %copy-start.64 = (bf16[1920,768]{1,0:T(8,128)(2,1)S(1)}, bf16[1920,768]{1,0:T(8,128)(2,1)}, u32[]{:S(2)}) copy-start(bf16[1920,768]{1,0:T(8,128)(2,1)} %get-tuple-element.134) | copy-start | bytes 8847364
  200.5 55.1 %reduce-scatter.23.cloned.1.call-start = ((), (), s32[]{:S(2)}) async-start(), calls=%async_computation.14 | async-start | bytes 2359296 | tf_op jit(solution)/shard_map/reduce_scatter | solution.py:367
  212.5 5.3 %copy-start.65 = (bf16[1920,768]{1,0:T(8,128)(2,1)S(1)}, bf16[1920,768]{1,0:T(8,128)(2,1)}, u32[]{:S(2)}) copy-start(bf16[1920,768]{1,0:T(8,128)(2,1)} %get-tuple-element.134) | copy-start | bytes 8847364
  212.5 5.3 %copy-start.90 = (f32[512,1536]{1,0:T(8,128)S(1)}, f32[512,1536]{1,0:T(8,128)}, u32[]{:S(2)}) copy-start(f32[512,1536]{1,0:T(8,128)} %copy-done.89) | copy-start | bytes 9437188
  214.4 10.5 %copy-start.6 = (f32[256,768]{1,0:T(8,128)}, f32[256,768]{1,0:T(8,128)S(1)}, u32[]{:S(2)}) copy-start(f32[256,768]{1,0:T(8,128)S(1)} %get-tuple-element.309) | copy-start | bytes 2359300
  217.8 4.4 copy-start.85
  224.8 33.8 %reduce-scatter.27.cloned.1.call-start = ((), (), s32[]{:S(2)}) async-start(), calls=%async_computation.16 | async-start | bytes 2359296 | tf_op jit(solution)/shard_map/reduce_scatter | solution.py:367
  227.3 5.5 %copy-start.59 = (bf16[512,768]{1,0:T(8,128)(2,1)}, bf16[512,768]{1,0:T(8,128)(2,1)S(1)}, u32[]{:S(2)}) copy-start(bf16[512,768]{1,0:T(8,128)(2,1)S(1)} %all_gather.38) | copy-start | bytes 2359300
  227.3 6.7 %copy-start.86 = (bf16[768,2688]{1,0:T(8,128)(2,1)S(1)}, bf16[768,2688]{1,0:T(8,128)(2,1)}, u32[]{:S(2)}) copy-start(bf16[768,2688]{1,0:T(8,128)(2,1)} %get-tuple-element.133) | copy-start | bytes 12386308
  233.9 5.0 %copy-start.20 = (bf16[512,768]{1,0:T(8,128)(2,1)S(1)}, bf16[512,768]{1,0:T(8,128)(2,1)}, u32[]{:S(2)}) copy-start(bf16[512,768]{1,0:T(8,128)(2,1)} %copy-done.19) | copy-start | bytes 2359300
  236.5 193.5 %reduce-scatter.31.cloned.1.call-start = ((), (), s32[]{:S(2)}) async-start(), calls=%async_computation.18 | async-start | bytes 1327104
  239.0 5.1 %copy-start.22 = (bf16[512,768]{1,0:T(8,128)(2,1)S(1)}, bf16[512,768]{1,0:T(8,128)(2,1)}, u32[]{:S(2)}) copy-start(bf16[512,768]{1,0:T(8,128)(2,1)} %copy-done.21) | copy-start | bytes 2359300
  239.0 5.1 %copy-start.38 = (bf16[512,1536]{1,0:T(8,128)(2,1)S(1)}, bf16[512,1536]{1,0:T(8,128)(2,1)}, u32[]{:S(2)}) copy-start(bf16[512,1536]{1,0:T(8,128)(2,1)} %copy-done.37) | copy-start | bytes 4718596
  255.5 11.7 %slice-start.2 = ((s8[6291456]{0:T(1024)(128)(4,1)}), s8[2097152]{0:T(1024)(128)(4,1)S(1)}, s32[]{:S(2)}) async-start(s8[6291456]{0:T(1024)(128)(4,1)} %bitcast.264), calls=%async_computation.22 | async-start | bytes 4194304
  258.6 8.7 %slice-start.3 = ((s8[6291456]{0:T(1024)(128)(4,1)}), s8[4194304]{0:T(1024)(128)(4,1)S(1)}, s32[]{:S(2)}) async-start(s8[6291456]{0:T(1024)(128)(4,1)} %bitcast.264), calls=%async_computation.23 | async-start | bytes 8388608
  272.4 8.5 %slice-start = ((s8[6291456]{0:T(1024)(128)(4,1)}), s8[4194304]{0:T(1024)(128)(4,1)S(1)}, s32[]{:S(2)}) async-start(s8[6291456]{0:T(1024)(128)(4,1)} %bitcast.262), calls=%async_computation.20 | async-start | bytes 8388608
  273.0 17.6 %copy-start.48 = (bf16[6,64,512]{2,1,0:T(8,128)(2,1)}, bf16[6,64,512]{2,1,0:T(8,128)(2,1)S(1)}, u32[]{:S(2)}) copy-start(bf16[6,64,512]{2,1,0:T(8,128)(2,1)S(1)} %fusion.50) | copy-start | bytes 1179652
  273.1 7.9 %slice-start.1 = ((s8[6291456]{0:T(1024)(128)(4,1)}), s8[2097152]{0:T(1024)(128)(4,1)S(1)}, s32[]{:S(2)}) async-start(s8[6291456]{0:T(1024)(128)(4,1)} %bitcast.262), calls=%async_computation.21 | async-start | bytes 4194304
  282.1 4.7 copy-start.46
  282.1 5.4 %copy-start.44 = (bf16[6,64,512]{2,1,0:T(8,128)(2,1)S(1)}, bf16[6,64,512]{2,1,0:T(8,128)(2,1)}, u32[]{:S(2)}) copy-start(bf16[6,64,512]{2,1,0:T(8,128)(2,1)} %fusion.54) | copy-start | bytes 1179652
  290.8 6.4 %copy-start.14 = (bf16[512,384]{0,1:T(8,128)(2,1)S(1)}, bf16[512,384]{0,1:T(8,128)(2,1)}, u32[]{:S(2)}) copy-start(bf16[512,384]{0,1:T(8,128)(2,1)} %copy-done.13) | copy-start | bytes 1179652
  300.4 141.4 %reduce-scatter.33.cloned.1.call-start = ((), (), s32[]{:S(2)}) async-start(), calls=%async_computation.19 | async-start | bytes 417792
  304.2 156.7 %reduce-scatter.25.cloned.1.call-start = ((), (), s32[]{:S(2)}) async-start(), calls=%async_computation.15 | async-start | bytes 2359296 | tf_op jit(solution)/shard_map/reduce_scatter | solution.py:367
  308.6 153.6 %reduce-scatter.29.cloned.1.call-start = ((), (), s32[]{:S(2)}) async-start(), calls=%async_computation.17 | async-start | bytes 2359296 | tf_op jit(solution)/shard_map/reduce_scatter | solution.py:367
  312.4 6.8 %copy-start.45 = (bf16[6,64,512]{2,1,0:T(8,128)(2,1)S(1)}, bf16[6,64,512]{2,1,0:T(8,128)(2,1)}, u32[]{:S(2)}) copy-start(bf16[6,64,512]{2,1,0:T(8,128)(2,1)} %fusion.54) | copy-start | bytes 1179652
  312.4 6.8 %copy-start.49 = (bf16[6,64,512]{2,1,0:T(8,128)(2,1)S(1)}, bf16[6,64,512]{2,1,0:T(8,128)(2,1)}, u32[]{:S(2)}) copy-start(bf16[6,64,512]{2,1,0:T(8,128)(2,1)} %copy-done.48) | copy-start | bytes 1179652
  312.4 6.8 %copy-start.54 = (bf16[1,1,512,768]{3,2,1,0:T(8,128)(2,1)S(1)}, bf16[1,1,512,768]{3,2,1,0:T(8,128)(2,1)}, u32[]{:S(2)}) copy-start(bf16[1,1,512,768]{3,2,1,0:T(8,128)(2,1)} %copy-done.53) | copy-start | bytes 2359300
  312.4 6.8 %copy-start.66 = (bf16[6,64,512]{2,1,0:T(8,128)(2,1)S(1)}, bf16[6,64,512]{2,1,0:T(8,128)(2,1)}, u32[]{:S(2)}) copy-start(bf16[6,64,512]{2,1,0:T(8,128)(2,1)} %fusion.51) | copy-start | bytes 1179652
  312.5 8.1 %copy-start.56 = (bf16[1,1,512,768]{3,2,1,0:T(8,128)(2,1)S(1)}, bf16[1,1,512,768]{3,2,1,0:T(8,128)(2,1)}, u32[]{:S(2)}) copy-start(bf16[1,1,512,768]{3,2,1,0:T(8,128)(2,1)} %copy-done.55) | copy-start | bytes 2359300
  324.7 98.2 %copy-start.29 = (f32[1,1,1,240,768]{4,3,2,1,0:T(8,128)S(1)}, f32[1,1,1,240,768]{4,3,2,1,0:T(8,128)}, u32[]{:S(2)}) copy-start(f32[1,1,1,240,768]{4,3,2,1,0:T(8,128)} %param.37) | copy-start | bytes 2211844
  324.7 98.2 %copy-start.30 = (f32[1,1,240,768]{3,2,1,0:T(8,128)S(1)}, f32[1,1,240,768]{3,2,1,0:T(8,128)}, u32[]{:S(2)}) copy-start(f32[1,1,240,768]{3,2,1,0:T(8,128)} %param.40) | copy-start | bytes 2211844
  324.7 98.2 %copy-start.61 = (f32[1,1,1,240,768]{4,3,2,1,0:T(8,128)S(1)}, f32[1,1,1,240,768]{4,3,2,1,0:T(8,128)}, u32[]{:S(2)}) copy-start(f32[1,1,1,240,768]{4,3,2,1,0:T(8,128)} %param.39) | copy-start | bytes 2211844
  324.8 98.2 %copy-start.62 = (f32[1,1,1,240,768]{4,3,2,1,0:T(8,128)S(1)}, f32[1,1,1,240,768]{4,3,2,1,0:T(8,128)}, u32[]{:S(2)}) copy-start(f32[1,1,1,240,768]{4,3,2,1,0:T(8,128)} %param.38) | copy-start | bytes 2211844
  425.8 5.2 %copy-start.78 = (f32[1,1,1,288]{3,2,1,0:T(1,128)S(1)}, f32[1,1,1,288]{3,2,1,0:T(1,128)}, u32[]{:S(2)}) copy-start(f32[1,1,1,288]{3,2,1,0:T(1,128)} %param.42) | copy-start | bytes 3460
  425.8 5.2 %copy-start.79 = (f32[1,1,288]{2,1,0:T(1,128)S(1)}, f32[1,1,288]{2,1,0:T(1,128)}, u32[]{:S(2)}) copy-start(f32[1,1,288]{2,1,0:T(1,128)} %param.45) | copy-start | bytes 3460
  425.8 5.2 %copy-start.81 = (f32[1,1,1,288]{3,2,1,0:T(1,128)S(1)}, f32[1,1,1,288]{3,2,1,0:T(1,128)}, u32[]{:S(2)}) copy-start(f32[1,1,1,288]{3,2,1,0:T(1,128)} %param.44) | copy-start | bytes 3460
  425.8 5.2 %copy-start.82 = (f32[1,1,1,288]{3,2,1,0:T(1,128)S(1)}, f32[1,1,1,288]{3,2,1,0:T(1,128)}, u32[]{:S(2)}) copy-start(f32[1,1,1,288]{3,2,1,0:T(1,128)} %param.43) | copy-start | bytes 3460
  425.8 7.7 %copy-start.10 = (f32[1,1,96,1,2688]{4,3,2,1,0:T(1,128)S(1)}, f32[1,1,96,1,2688]{4,3,2,1,0:T(1,128)}, u32[]{:S(2)}) copy-start(f32[1,1,96,1,2688]{4,3,2,1,0:T(1,128)} %param.32) | copy-start | bytes 3096580
  425.8 7.7 %copy-start.11 = (f32[96,2688]{1,0:T(8,128)S(1)}, f32[96,2688]{1,0:T(8,128)}, u32[]{:S(2)}) copy-start(f32[96,2688]{1,0:T(8,128)} %get-tuple-element.135) | copy-start | bytes 3096580
  425.8 7.7 %copy-start.12 = (f32[1,96,1,2688]{3,2,1,0:T(1,128)S(1)}, f32[1,96,1,2688]{3,2,1,0:T(1,128)}, u32[]{:S(2)}) copy-start(f32[1,96,1,2688]{3,2,1,0:T(1,128)} %param.35) | copy-start | bytes 3096580
  425.8 24.7 %collective-permute-start.1 = (bf16[1,1,240,768]{3,2,1,0:T(8,128)(2,1)S(1)}, bf16[1,1,240,768]{3,2,1,0:T(8,128)(2,1)}, u32[]{:S(2)}, u32[]{:S(2)}) collective-permute-start(bf16[1,1,240,768]{3,2,1,0:T(8,128)(2,1)S(1)} %get-tuple-element.325), channel_id=1, source_target_pairs={{0,16},{16,0},{1,17},{17,1},{2,18},{18,2},{3,19},{19,3},{4,20},{20... | collective-permute-start | bytes 1105928 | tf_op jit(solution)/shard_map/ppermute | solution.py:765
  431.0 6.1 %copy-start.75 = (f32[1,288]{1,0:T(1,128)}, f32[1,288]{1,0:T(1,128)S(1)}, u32[]{:S(2)}) copy-start(f32[1,288]{1,0:T(1,128)S(1)} %copy.237) | copy-start | bytes 3460
  431.6 9.6 %collective-permute-start.2 = (bf16[1,1,288]{2,1,0:T(2,128)(2,1)S(1)}, bf16[1,1,288]{2,1,0:T(2,128)(2,1)S(1)}, u32[]{:S(2)}, u32[]{:S(2)}) collective-permute-start(bf16[1,1,288]{2,1,0:T(2,128)(2,1)S(1)} %get-tuple-element.319), channel_id=1, source_target_pairs={{0,16},{16,0},{1,17},{17,1},{2,18},{18,2},{3,19},{19,3},{4,20},{20... | collective-permute-start | bytes 1736 | tf_op jit(solution)/shard_map/ppermute | solution.py:765
  437.1 4.1 copy-start.83
  437.1 5.7 %copy-start.71 = (f32[1,1,6,48]{3,1,2,0:T(1,128)S(1)}, f32[1,1,6,48]{3,1,2,0:T(1,128)}, u32[]{:S(2)}) copy-start(f32[1,1,6,48]{3,1,2,0:T(1,128)} %param.47) | copy-start | bytes 3460
  437.1 5.7 %copy-start.72 = (f32[1,1,6,48]{3,1,2,0:T(1,128)S(1)}, f32[1,1,6,48]{3,1,2,0:T(1,128)}, u32[]{:S(2)}) copy-start(f32[1,1,6,48]{3,1,2,0:T(1,128)} %param.49) | copy-start | bytes 3460
  437.1 5.7 %copy-start.73 = (f32[1,1,6,48]{3,1,2,0:T(1,128)S(1)}, f32[1,1,6,48]{3,1,2,0:T(1,128)}, u32[]{:S(2)}) copy-start(f32[1,1,6,48]{3,1,2,0:T(1,128)} %param.48) | copy-start | bytes 3460
  437.1 5.7 %copy-start.74 = (f32[1,6,48]{2,0,1:T(1,128)S(1)}, f32[1,6,48]{2,0,1:T(1,128)}, u32[]{:S(2)}) copy-start(f32[1,6,48]{2,0,1:T(1,128)} %param.50) | copy-start | bytes 3460
  437.1 12.8 %copy-start.80 = (f32[1,6,48]{2,0,1:T(1,128)S(1)}, f32[1,6,48]{2,0,1:T(1,128)}, u32[]{:S(2)}) copy-start(f32[1,6,48]{2,0,1:T(1,128)} %param.51) | copy-start | bytes 3460
  437.2 13.3 %copy-start.31 = (f32[1,1,240,768]{3,2,1,0:T(8,128)S(1)}, f32[1,1,240,768]{3,2,1,0:T(8,128)}, u32[]{:S(2)}) copy-start(f32[1,1,240,768]{3,2,1,0:T(8,128)} %param.40) | copy-start | bytes 2211844
  439.2 14.1 %collective-permute-start = (bf16[1,96,1,2688]{3,1,2,0:T(8,128)(2,1)}, bf16[1,96,1,2688]{3,1,2,0:T(8,128)(2,1)}, u32[]{:S(2)}, u32[]{:S(2)}) collective-permute-start(bf16[1,96,1,2688]{3,1,2,0:T(8,128)(2,1)} %get-tuple-element.328), channel_id=1, source_target_pairs={{0,16},{16,0},{1,17},{17,1},{2,18},{18,2},{3,19},{19,3},{4,20},{20... | collective-permute-start | bytes 1548296 | tf_op jit(solution)/shard_map/ppermute | solution.py:765
  439.2 14.1 %copy-start.52 = (f32[1,96,1,2688]{3,2,1,0:T(1,128)S(1)}, f32[1,96,1,2688]{3,2,1,0:T(1,128)}, u32[]{:S(2)}) copy-start(f32[1,96,1,2688]{3,2,1,0:T(1,128)} %param.36) | copy-start | bytes 3096580
  442.8 12.0 %copy-start.67 = (f32[1,6,48]{2,0,1:T(1,128)}, f32[1,6,48]{2,0,1:T(1,128)S(1)}, u32[]{:S(2)}) copy-start(f32[1,6,48]{2,0,1:T(1,128)S(1)} %copy.239) | copy-start | bytes 3460
  442.9 7.0 %collective-permute-start.3 = (bf16[1,6,48]{2,0,1:T(2,128)(2,1)S(1)}, bf16[1,6,48]{2,0,1:T(2,128)(2,1)S(1)}, u32[]{:S(2)}, u32[]{:S(2)}) collective-permute-start(bf16[1,6,48]{2,0,1:T(2,128)(2,1)S(1)} %fusion.112), channel_id=1, source_target_pairs={{0,16},{16,0},{1,17},{17,1},{2,18},{18,2},{3,19},{19,3},{4,20},{20... | collective-permute-start | bytes 1736 | tf_op jit(solution)/shard_map/ppermute | solution.py:765
  454.8 6.1 %copy-start.8 = (f32[256,768]{1,0:T(8,128)S(1)}, f32[256,768]{1,0:T(8,128)}, u32[]{:S(2)}) copy-start(f32[256,768]{1,0:T(8,128)} %copy-done.7) | copy-start | bytes 2359300
  456.9 5.3 %copy-start.5 = (f32[256,768]{1,0:T(8,128)S(1)}, f32[256,768]{1,0:T(8,128)}, u32[]{:S(2)}) copy-start(f32[256,768]{1,0:T(8,128)} %copy-done.4) | copy-start | bytes 2359300
  (50 other events, 113.6 us)
Sparse Core Ops, SparseCore 0:
  138.9 8.9 reduce-scatter.14
  155.0 8.9 reduce-scatter.18
  189.6 6.3 reduce-scatter.20
  200.6 8.3 reduce-scatter.16
  224.9 10.2 reduce-scatter.22
  238.0 10.2 reduce-scatter.26
  300.5 68.0 reduce-scatter.30
  372.2 55.0 reduce-scatter.32
  429.6 8.0 reduce-scatter.24
  440.4 10.2 reduce-scatter.28

commit v2 on v0

--- a/solution.py
+++ b/solution.py
@@ -1,6 +1,8 @@
 import jax
 import jax.numpy as jnp
 from jax import lax
+from jax.experimental import pallas as pl
+from jax.experimental.pallas import tpu as pltpu
 from jax.sharding import PartitionSpec as P
 
 BETA_ONE = 0.9
@@ -12,6 +14,850 @@
 OUTER_RATE = 0.7
 NORM_EPS = 1e-06
 MASKED = -1e30
+MESH = pl.DeviceIdType.MESH
+ZS = 4
+F32, BF16 = jnp.float32, jnp.bfloat16
+
+
+def place():
+    d = lax.axis_index("dp")
+    return d // 2, lax.rem(d, 2)
+
+
+def neighbours():
+    g, t = lax.axis_index("group"), lax.axis_index("tensor")
+    z, x = place()
+    return dict(
+        x=(g, z * 2 + (1 - x), t),
+        up=(g, (z + 1) * 2 + x, t),
+        down=(g, (z - 1) * 2 + x, t),
+        core=(g, z * 2 + x, 1 - t),
+        group=(1 - g, z * 2 + x, t),
+    )
+
+
+def entry_barrier():
+    z, _ = place()
+    near = neighbours()
+    bar = pltpu.get_barrier_semaphore()
+
+    def greet(name):
+        pl.semaphore_signal(bar, inc=1, device_id=near[name], device_id_type=MESH)
+
+    for name in ("x", "core", "group"):
+        greet(name)
+    pl.when(z < ZS - 1)(lambda: greet("up"))
+    pl.when(z > 0)(lambda: greet("down"))
+    pl.semaphore_wait(bar, 3 + (z + 2) // 3 + (ZS + 1 - z) // 3)
+
+
+WAYS = {"x": 0, "up": 1, "down": 2}
+
+
+class Gather:
+    def __init__(self, view, ssem, rsem):
+        self.view, self.ssem, self.rsem = view, ssem, rsem
+        self.near = neighbours()
+        self.z, self.x = place()
+
+    def copy(self, g, zsrc, xsrc, way):
+        ref = self.view(g, zsrc * 2 + xsrc)
+        return pltpu.make_async_remote_copy(
+            src_ref=ref,
+            dst_ref=ref,
+            send_sem=self.ssem.at[g, zsrc, WAYS[way]],
+            recv_sem=self.rsem.at[g, zsrc * 2 + xsrc],
+            device_id=self.near[way],
+            device_id_type=MESH,
+        )
+
+    def own(self, g, only=None):
+        z, x = self.z, self.x
+        ok = (z >= 0) if only is None else only(z)
+        pl.when(ok)(lambda: self.copy(g, z, x, "x").start())
+        pl.when(ok & (z < ZS - 1))(lambda: self.copy(g, z, x, "up").start())
+        pl.when(ok & (z > 0))(lambda: self.copy(g, z, x, "down").start())
+
+    def relay(self, g, k, only=None):
+        z, x = self.z, self.x
+        for way, src in (("up", z - k), ("down", z + k)):
+            ok = (src >= 0) if way == "up" else (src < ZS)
+            if only is not None:
+                ok = ok & only(src)
+            more = (z < ZS - 1) if way == "up" else (z > 0)
+
+            @pl.when(ok)
+            def _():
+                self.copy(g, src, x, way).wait_recv()
+                self.copy(g, src, x, "x").start()
+                pl.when(more)(lambda: self.copy(g, src, x, way).start())
+
+    def across(self, g, srcs=range(ZS)):
+        for zsrc in srcs:
+            self.copy(g, zsrc, 1 - self.x, "x").wait_recv()
+
+    def drain(self, g, srcs=range(ZS)):
+        z, x = self.z, self.x
+        for zsrc in srcs:
+            self.copy(g, zsrc, x, "x").wait_send()
+            pl.when((zsrc <= z) & (z < ZS - 1))(lambda: self.copy(g, zsrc, x, "up").wait_send())
+            pl.when((zsrc >= z) & (z > 0))(lambda: self.copy(g, zsrc, x, "down").wait_send())
+
+
+def far_order(z, k):
+    if k == 0:
+        return 3 * (1 - z // 2)
+    if k == 1:
+        return lax.rem(2 + 3 * z, 5)
+    if k == 2:
+        return 1 + lax.rem(z, 2)
+    return z
+
+
+class Scatter:
+    def __init__(self, source, xbuf, zbuf, xs, xr, zs, zr):
+        self.source, self.xbuf, self.zbuf = source, xbuf, zbuf
+        self.xs, self.xr, self.zs, self.zr = xs, xr, zs, zr
+        self.near = neighbours()
+        self.z, self.x = place()
+
+    def xcopy(self, g, row):
+        return pltpu.make_async_remote_copy(
+            src_ref=self.source(g, row * 2 + (1 - self.x)),
+            dst_ref=self.xbuf(g, row),
+            send_sem=self.xs.at[g, row],
+            recv_sem=self.xr.at[g, row],
+            device_id=self.near["x"],
+            device_id_type=MESH,
+        )
+
+    def zcopy(self, g, row, slot, way):
+        return pltpu.make_async_remote_copy(
+            src_ref=self.xbuf(g, row),
+            dst_ref=self.zbuf(g, slot),
+            send_sem=self.zs.at[g, row],
+            recv_sem=self.zr.at[g, slot],
+            device_id=self.near[way],
+            device_id_type=MESH,
+        )
+
+    def send(self, g, k, only=None):
+        row = far_order(self.z, k)
+        ok = (row >= 0) if only is None else only(row)
+        pl.when(ok)(lambda: self.xcopy(g, row).start())
+
+    def pass_on(self, g, k, only=None):
+        z, x = self.z, self.x
+        row = far_order(z, k)
+        ok = (row >= 0) if only is None else only(row)
+
+        @pl.when(ok)
+        def _():
+            self.xcopy(g, row).wait_recv()
+            below = z < row
+            further = (below & (z > 0)) | ((z > row) & (z < ZS - 1))
+            src, buf = self.source(g, row * 2 + x), self.xbuf(g, row)
+
+            def add(*others):
+                def body(i, _):
+                    at = pl.ds(pl.multiple_of(i * 48, 48), 48)
+                    total = buf[at, :].astype(F32)
+                    for other in others:
+                        total = total + other[at, :].astype(F32)
+                    buf[at, :] = total.astype(BF16)
+                    return 0
+
+                lax.fori_loop(0, buf.shape[0] // 48, body, 0)
+
+            @pl.when(further)
+            def _():
+                self.zcopy(g, row, row, "up").wait_recv()
+                add(src, self.zbuf(g, row))
+
+            @pl.when(jnp.logical_not(further))
+            def _():
+                add(src)
+
+            pl.when(below & (z + 1 < row))(lambda: self.zcopy(g, row, row, "up").start())
+            pl.when(below & (z + 1 == row))(lambda: self.zcopy(g, row, ZS, "up").start())
+            pl.when(z > row)(lambda: self.zcopy(g, row, row, "down").start())
+
+    def arrived(self, g):
+        z = self.z
+        self.xcopy(g, z).wait_recv()
+        pl.when(z < ZS - 1)(lambda: self.zcopy(g, z, z, "down").wait_recv())
+        pl.when(z > 0)(lambda: self.zcopy(g, z, ZS, "up").wait_recv())
+
+    def drain(self, g, k, only=None):
+        row = far_order(self.z, k)
+        ok = (row >= 0) if only is None else only(row)
+
+        @pl.when(ok)
+        def _():
+            self.xcopy(g, row).wait_send()
+            if k < 3:
+                self.zcopy(g, row, row, "up").wait_send()
+
+
+VMEM_SPEC = pl.BlockSpec(memory_space=pltpu.VMEM)
+SMEM_SPEC = pl.BlockSpec(memory_space=pltpu.SMEM)
+ANY_SPEC = pl.BlockSpec(memory_space=pl.ANY)
+DMA = pltpu.SemaphoreType.DMA
+BIG_VMEM = 61 * 1024 * 1024
+LANE = 128
+GQKV, GUP, GNAR, GSMALL, GSUMS = range(5)
+
+
+def mm(left, right, left_dim, right_dim):
+    return lax.dot_general(
+        left, right, (((left_dim,), (right_dim,)), ((), ())), preferred_element_type=F32
+    )
+
+
+def span(start, size, multiple):
+    return pl.ds(pl.multiple_of(start, multiple), size)
+
+
+def by_eights(values):
+    rows, cols = values.shape
+    return jnp.sum(values.reshape(rows // 8, 8, cols), axis=0)
+
+
+def first_row(row):
+    return row == 0
+
+
+def other_rows(row):
+    return row > 0
+
+
+class Sizes:
+    def __init__(self, x, wide_own, narrow_own, rand):
+        self.micro, self.own, self.d = x.shape
+        self.seq = 2 * self.own
+        self.heads = rand.shape[1]
+        self.dt = self.heads * 64
+        self.ft = 2 * self.d
+        self.wr = self.d // 8
+        self.nr = narrow_own.shape[0]
+        self.wc = 3 * self.dt + self.ft
+        self.tiles = self.wc // LANE
+        self.tokens = self.micro * self.seq
+
+
+def layer_kernel(sz, *refs):
+    (
+        x_in, cot_in, lens, glob, rand, consts, small, w_lin, w_nar,
+        f_lin, s_lin, a_lin, f_nar, s_nar, a_nar,
+        out_ref, ingrad_ref, glin_out, gnar_out, mlin_out, mnar_out, small_out,
+        wide, nar, xf, cot, qkv, mix, dmix, lse, mask, blocks,
+        ps, pr, normed, scal, in2, uu, zb, drb, res, stage,
+        gw, gn, xw, xn, zw, zn, glin, gnar, mlin, mnar, wn32,
+        dsw, dsn, drw, drn, sm_all, sg_all, sm_mine, sm_peer, bias_row, norm_row, acc_b, acc_n,
+        gsend, grecv, xs, xr, zs, zr, core_s, core_r, ys, yr, loc,
+    ) = refs
+    z, x = place()
+    shard = z * 2 + x
+    t = lax.axis_index("tensor")
+    near = neighbours()
+    D, DT, FT, OWN, SEQ, WR, NR = sz.d, sz.dt, sz.ft, sz.own, sz.seq, sz.wr, sz.nr
+    QC = 3 * DT
+    own_at = span(t * OWN, OWN, OWN)
+    peer_at = span((1 - t) * OWN, OWN, OWN)
+
+    def local(src, dst, sem):
+        return pltpu.make_async_copy(src, dst, loc.at[sem])
+
+    loads = [
+        local(w_lin, uu.at[pl.ds(0, sz.tiles * WR)], 0),
+        local(w_nar, wn32, 1),
+        local(x_in.at[0], xf.at[0, own_at], 2),
+        local(x_in.at[1], xf.at[1, own_at], 3),
+        local(cot_in, cot, 4),
+    ]
+    for copy in loads:
+        copy.start()
+    entry_barrier()
+
+    def halves(g):
+        return pl.ds(0, QC) if g == GQKV else pl.ds(QC, FT)
+
+    def view(g, s):
+        if g == GNAR:
+            return nar.at[span(s * NR, NR, NR)]
+        if g == GSMALL:
+            return sm_all.at[s]
+        if g == GSUMS:
+            return sg_all.at[s]
+        return wide.at[span(s * WR, WR, WR), halves(g)]
+
+    gat = Gather(view, gsend, grecv)
+
+    def source(g, s):
+        if g == GNAR:
+            return gn.at[span(s * NR, NR, NR)]
+        return gw.at[span(s * WR, WR, WR), halves(g)]
+
+    sca = Scatter(
+        source,
+        lambda g, row: xn.at[row] if g == GNAR else xw.at[row, :, halves(g)],
+        lambda g, row: zn.at[row] if g == GNAR else zw.at[row, :, halves(g)],
+        xs, xr, zs, zr,
+    )
+
+    def core_copy(stage_at, src, dst):
+        return pltpu.make_async_remote_copy(
+            src_ref=src, dst_ref=dst, send_sem=core_s.at[stage_at], recv_sem=core_r.at[stage_at],
+            device_id=near["core"], device_id_type=MESH,
+        )
+
+    def rows_copy(kind, m, ref):
+        return core_copy(kind * 2 + m, ref.at[span(m * SEQ + t * OWN, OWN, OWN)],
+                         ref.at[span(m * SEQ + t * OWN, OWN, OWN)])
+
+    def part_copy(kind, m):
+        return core_copy(kind * 2 + m, ps.at[m], pr.at[m])
+
+    def x_copy(m):
+        return core_copy(m, x_in.at[m], xf.at[m, own_at])
+
+    for m in range(2):
+        x_copy(m).start()
+
+    sm_all[shard] = small[...]
+    gat.own(GSMALL)
+    loads[0].wait()
+
+    def cast_tiles(lo, hi):
+        def body(c, _):
+            wide[span(shard * WR, WR, WR), span(c * LANE, LANE, LANE)] = uu[
+                pl.ds(c, WR, stride=sz.tiles), :
+            ].astype(BF16)
+            return 0
+
+        lax.fori_loop(lo, hi, body, 0)
+
+    cast_tiles(0, QC // LANE)
+    gat.own(GQKV)
+    loads[1].wait()
+    nar[span(shard * NR, NR, NR), :] = wn32[...].astype(BF16)
+    gat.own(GNAR, first_row)
+    cast_tiles(QC // LANE, sz.tiles)
+
+    def build_masks():
+        keys = lax.broadcasted_iota(jnp.int32, (SEQ, LANE), 0)
+        lanes = lax.broadcasted_iota(jnp.int32, (SEQ, LANE), 1)
+        kb = keys // 64
+        blocks[...] = (kb == lanes).astype(F32).astype(BF16)
+        for m in range(2):
+            g0, g1 = glob[m, 0], glob[m, 1]
+            base = (jnp.abs(kb - lanes) <= 1) | (kb == g0) | (kb == g1) | (lanes == g0) | (lanes == g1)
+            real = keys < lens[m]
+
+            def body(h, _):
+                rows = rand[m, h]
+                hit = base
+                for r in range(3):
+                    hit = hit | (kb == rows[r : r + 1, :])
+                mask[m * sz.heads + h] = jnp.where(hit & real, 0.0, MASKED).astype(BF16)
+                return 0
+
+            lax.fori_loop(0, sz.heads, body, 0)
+
+    gat.relay(GSMALL, 1)
+    gat.relay(GQKV, 1)
+    gat.own(GUP)
+    build_masks()
+    gat.relay(GSMALL, 2)
+    gat.relay(GQKV, 2)
+    gat.relay(GSMALL, 3)
+    gat.relay(GQKV, 3)
+    gat.relay(GNAR, 1, first_row)
+
+    gat.across(GSMALL)
+    total = sm_all[0].astype(F32)
+    for s in range(1, 8):
+        total = total + sm_all[s].astype(F32)
+    sm_mine[...] = total
+
+    def small_copy():
+        return core_copy(2, sm_mine, sm_peer)
+
+    small_copy().start()
+    nb = bias_row.shape[1] // LANE
+    small_copy().wait_recv()
+    for c in range(nb):
+        bias_row[0:1, c * LANE : (c + 1) * LANE] = sm_mine[c : c + 1, :]
+    both = sm_mine[...] + sm_peer[...]
+    for r in range(6):
+        for c in range(D // LANE):
+            at = nb + r * (D // LANE) + c
+            norm_row[r : r + 1, c * LANE : (c + 1) * LANE] = both[at : at + 1, :]
+    acc_b[...] = jnp.zeros_like(acc_b)
+    acc_n[...] = jnp.zeros_like(acc_n)
+
+    gat.across(GQKV)
+    for m in range(2):
+        loads[2 + m].wait()
+        x_copy(m).wait_recv()
+        for c in range(3):
+            value = mm(xf[m], wide[:, c * DT : (c + 1) * DT], 1, 0)
+            if c != 1:
+                lo = 0 if c == 0 else DT
+                value = value + bias_row[0:1, lo : lo + DT]
+            qkv[m, :, c * DT : (c + 1) * DT] = value.astype(BF16)
+        if m == 0:
+            gat.relay(GNAR, 2, first_row)
+
+    lane_low = lax.broadcasted_iota(jnp.int32, (1, LANE), 1) < 64
+
+    def half(value, hh):
+        return jnp.where(lane_low if hh == 0 else jnp.logical_not(lane_low), value, jnp.zeros_like(value))
+
+    def pair_loads(m, p):
+        return [qkv[m, :, span(c * DT + p * LANE, LANE, LANE)] for c in range(3)]
+
+    def scores(m, p, hh, q, kh):
+        head = m * sz.heads + p * 2 + hh
+        kx = jnp.concatenate([kh, mask[head]], axis=1)
+        qx = jnp.concatenate([q * jnp.asarray(0.125, BF16), blocks[...]], axis=1)
+        return mm(kx, qx, 1, 1), head
+
+    def attend(m):
+        def body(p, _):
+            q, k, v = pair_loads(m, p)
+            out_t = jnp.zeros((LANE, SEQ), F32)
+            for hh in range(2):
+                s, head = scores(m, p, hh, q, half(k, hh))
+                top = jnp.max(s, axis=0, keepdims=True)
+                e = jnp.exp(s - top)
+                total_e = jnp.sum(e, axis=0, keepdims=True)
+                prob = (e * (1.0 / total_e)).astype(BF16)
+                lse[head] = jnp.broadcast_to(top + jnp.log(total_e), (8, SEQ))
+                out_t = out_t + mm(half(v, hh), prob, 0, 0)
+            mix[span(m * SEQ, SEQ, SEQ), span(p * LANE, LANE, LANE)] = jnp.transpose(out_t).astype(BF16)
+            return 0
+
+        lax.fori_loop(0, sz.heads // 2, body, 0)
+
+    gat.relay(GUP, 1)
+    gat.own(GNAR, other_rows)
+    attend(0)
+    gat.relay(GNAR, 3, first_row)
+    gat.relay(GUP, 2)
+    attend(1)
+    gat.relay(GUP, 3)
+
+    def branch(m, left, right, right_dim, kind, add):
+        value = mm(left[span(m * SEQ + (1 - t) * OWN, OWN, OWN), :], right, 1, right_dim)
+        ps[m] = value
+        part_copy(PARTS[kind], m).start()
+        value = mm(left[span(m * SEQ + t * OWN, OWN, OWN), :], right, 1, right_dim)
+        if add:
+            res[m] += value
+        else:
+            res[m] = value
+
+    gat.across(GNAR, [0])
+    for m in range(2):
+        branch(m, mix, nar[0:DT, :], 0, 0, False)
+
+    def rows_loop(body):
+        lax.fori_loop(0, OWN // 64, lambda i, c: (body(span(i * 64, 64, 64), i * 64), c)[1], 0)
+
+    def stats(r):
+        mean = jnp.mean(r, axis=1, keepdims=True)
+        centred = r - mean
+        var = jnp.mean(centred * centred, axis=1, keepdims=True)
+        scaling = lax.rsqrt(var + NORM_EPS)
+        return centred * scaling, scaling
+
+    def norm(r):
+        return norm_row[r : r + 1, :]
+
+    def norm_one(m):
+        part_copy(PARTS[0], m).wait()
+
+        def body(rows, at):
+            hidden = xf[m, span(t * OWN + at, 64, 64), :].astype(F32)
+            n, scaling = stats(hidden + (res[m, rows, :] + pr[m, rows, :]) + norm(0))
+            normed[m, rows, :] = n
+            scal[m, rows, :] = scaling
+            in2[span(m * SEQ + t * OWN + at, 64, 64), :] = (n * norm(2) + norm(3)).astype(BF16)
+
+        rows_loop(body)
+        rows_copy(ROWS[0], m, in2).start()
+
+    for m in range(2):
+        norm_one(m)
+    gat.relay(GNAR, 1, other_rows)
+
+    gat.across(GUP)
+
+    def feed(m):
+        rows_copy(ROWS[0], m, in2).wait()
+
+        def body(c, _):
+            value = mm(
+                in2[span(m * SEQ, SEQ, SEQ), :], wide[:, span(QC + c * 256, 256, LANE)], 1, 0
+            ) + bias_row[0:1, span(2 * DT + c * 256, 256, LANE)]
+            square = value * value
+            inner = GELU_A * value * (1.0 + GELU_B * square)
+            tan = jnp.tanh(inner)
+            hat = 0.5 * (1.0 + tan)
+            zb[span(m * SEQ, SEQ, SEQ), span(c * 256, 256, 256)] = (value * hat).astype(BF16)
+            slope = hat + 0.5 * value * (1.0 - tan * tan) * (GELU_A * (1.0 + 3.0 * GELU_B * square))
+            for j in range(2):
+                uu[span((c * 2 + j) * sz.tokens + m * SEQ, SEQ, SEQ), :] = slope[:, j * LANE : (j + 1) * LANE]
+            return 0
+
+        lax.fori_loop(0, FT // 256, body, 0)
+
+    feed(0)
+    gat.relay(GNAR, 2, other_rows)
+    feed(1)
+    gat.relay(GNAR, 3, other_rows)
+    gat.across(GNAR, [1, 2, 3])
+    for m in range(2):
+        branch(m, zb, nar[DT:, :], 0, 1, False)
+
+    loads[4].wait()
+
+    def count(kind, value):
+        acc_n[kind] += by_eights(value)
+
+    def norm_back(grad, n, scaling, gain):
+        scaled = grad * gain
+        return scaling * (
+            scaled
+            - jnp.mean(scaled, axis=1, keepdims=True)
+            - n * jnp.mean(scaled * n, axis=1, keepdims=True)
+        )
+
+    def norm_two(m):
+        part_copy(PARTS[1], m).wait()
+
+        def body(rows, at):
+            first = normed[m, rows, :] * norm(2) + norm(3)
+            n, scaling = stats(first + (res[m, rows, :] + pr[m, rows, :]) + norm(1))
+            stage[m, rows, :] = n * norm(4) + norm(5)
+            token = t * OWN + at + lax.broadcasted_iota(jnp.int32, (64, 1), 0)
+            grad = jnp.where(token < lens[m], cot[m, rows, :].astype(F32), 0.0)
+            count(4, grad * n)
+            count(5, grad)
+            back = norm_back(grad, n, scaling, norm(4))
+            count(1, back)
+            res[m, rows, :] = back
+            drb[span(m * SEQ + t * OWN + at, 64, 64), :] = back.astype(BF16)
+
+        rows_loop(body)
+        rows_copy(ROWS[1], m, drb).start()
+
+    def out_copy(m):
+        return local(stage.at[m], out_ref.at[m], 5 + m)
+
+    for m in range(2):
+        norm_two(m)
+        out_copy(m).start()
+
+    for m in range(2):
+        rows_copy(ROWS[1], m, drb).wait()
+
+    def down_grad(c, _):
+        gn[span(DT + c * 256, 256, LANE), :] = mm(zb[:, span(c * 256, 256, 256)], drb[...], 0, 0).astype(BF16)
+        return 0
+
+    lax.fori_loop(0, FT // 256, down_grad, 0)
+    for k in range(4):
+        sca.send(GNAR, k, other_rows)
+
+    def feed_back(m):
+        def body(c, _):
+            grad = mm(
+                drb[span(m * SEQ, SEQ, SEQ), :], nar[span(DT + c * 256, 256, LANE), :], 1, 1
+            )
+            slope = jnp.concatenate(
+                [uu[span((c * 2 + j) * sz.tokens + m * SEQ, SEQ, SEQ), :] for j in range(2)], axis=1
+            )
+            low = (grad * slope).astype(BF16)
+            zb[span(m * SEQ, SEQ, SEQ), span(c * 256, 256, 256)] = low
+            acc_b[:, span(2 * DT + c * 256, 256, LANE)] += by_eights(low.astype(F32))
+            return 0
+
+        lax.fori_loop(0, FT // 256, body, 0)
+
+    for m in range(2):
+        feed_back(m)
+
+    def up_grad(c, _):
+        gw[span(c * 256, 256, 256), QC:] = mm(in2[:, span(c * 256, 256, 256)], zb[...], 0, 0).astype(BF16)
+        return 0
+
+    lax.fori_loop(0, D // 256, up_grad, 0)
+    for k in range(4):
+        sca.send(GUP, k)
+
+    base = 3 * sz.tiles * WR
+    tiles_n = D // LANE
+    states = []
+    for at, (lin, flat) in enumerate(((f_lin, f_nar), (s_lin, s_nar), (a_lin, a_nar))):
+        states.append(local(lin, uu.at[pl.ds(at * sz.tiles * WR, sz.tiles * WR)], 7 + at))
+        for c in range(tiles_n):
+            states.append(
+                local(
+                    flat.at[:, pl.ds(c * LANE, LANE)],
+                    uu.at[pl.ds(base + (at * tiles_n + c) * NR, NR)],
+                    10 + at * tiles_n + c,
+                )
+            )
+    states.append(local(w_lin, glin, 10 + 3 * tiles_n))
+    for copy in states:
+        copy.start()
+
+    for m in range(2):
+        branch(m, zb, wide[:, QC:], 1, 2, True)
+    sca.pass_on(GNAR, 0, other_rows)
+
+    def norm_one_back(m):
+        part_copy(PARTS[2], m).wait()
+
+        def body(rows, at):
+            grad = res[m, rows, :] + pr[m, rows, :]
+            n = normed[m, rows, :]
+            count(2, grad * n)
+            count(3, grad)
+            back = norm_back(grad, n, scal[m, rows, :], norm(2))
+            count(0, back)
+            res[m, rows, :] = back
+            drb[span(m * SEQ + t * OWN + at, 64, 64), :] = back.astype(BF16)
+
+        rows_loop(body)
+        rows_copy(ROWS[2], m, drb).start()
+
+    for m in range(2):
+        norm_one_back(m)
+    for m in range(2):
+        rows_copy(ROWS[2], m, drb).wait()
+    gn[0:DT, :] = mm(mix[...], drb[...], 0, 0).astype(BF16)
+    for k in range(4):
+        sca.send(GNAR, k, first_row)
+    for m in range(2):
+        dmix[span(m * SEQ, SEQ, SEQ), :] = mm(
+            drb[span(m * SEQ, SEQ, SEQ), :], nar[0:DT, :], 1, 1
+        ).astype(BF16)
+    sca.pass_on(GNAR, 1, other_rows)
+
+    def attend_back(m):
+        def body(p, _):
+            q, k, v = pair_loads(m, p)
+            do = dmix[span(m * SEQ, SEQ, SEQ), span(p * LANE, LANE, LANE)]
+            dq_t = jnp.zeros((LANE, SEQ), F32)
+            dk = jnp.zeros((SEQ, LANE), F32)
+            dv = jnp.zeros((SEQ, LANE), F32)
+            for hh in range(2):
+                kh = half(k, hh)
+                s, head = scores(m, p, hh, q, kh)
+                prob = jnp.exp(s - lse[head][0:1, :])
+                dp = mm(half(v, hh), do, 1, 1)
+                centre = jnp.sum(prob * dp, axis=0, keepdims=True)
+                ds = (prob * (dp - centre)).astype(BF16)
+                dq_t = dq_t + mm(kh, ds, 0, 0)
+                dk = dk + mm(ds, half(q, hh), 1, 0)
+                dv = dv + mm(prob.astype(BF16), half(do, hh), 1, 0)
+            for c, value in enumerate((jnp.transpose(dq_t) * 0.125, dk * 0.125, dv)):
+                low = value.astype(BF16)
+                qkv[m, :, span(c * DT + p * LANE, LANE, LANE)] = low
+                if c != 1:
+                    lo = 0 if c == 0 else DT
+                    acc_b[:, span(lo + p * LANE, LANE, LANE)] += by_eights(low.astype(F32))
+            return 0
+
+        lax.fori_loop(0, sz.heads // 2, body, 0)
+
+    attend_back(0)
+    sca.pass_on(GNAR, 2, other_rows)
+    attend_back(1)
+    sca.pass_on(GUP, 0)
+
+    def attn_grad(c, _):
+        value = mm(xf[0, :, span(c * 256, 256, 256)], qkv[0], 0, 0)
+        value = value + mm(xf[1, :, span(c * 256, 256, 256)], qkv[1], 0, 0)
+        gw[span(c * 256, 256, 256), 0:QC] = value.astype(BF16)
+        return 0
+
+    lax.fori_loop(0, D // 256, attn_grad, 0)
+    for k in range(4):
+        sca.send(GQKV, k)
+
+    sums = sg_all.at[shard]
+    sums[...] = jnp.zeros((sg_all.shape[1], LANE), F32)
+    flat = jnp.sum(acc_b[...], axis=0, keepdims=True)
+    for c in range(nb):
+        sums[c : c + 1, :] = flat[:, c * LANE : (c + 1) * LANE]
+    for r in range(6):
+        flat = jnp.sum(acc_n[r], axis=0, keepdims=True)
+        for c in range(tiles_n):
+            at = nb + r * tiles_n + c
+            sums[at : at + 1, :] = flat[:, c * LANE : (c + 1) * LANE]
+    gat.own(GSUMS)
+
+    for m in range(2):
+        out_copy(m).wait()
+
+    def qkv_branch(m):
+        right = wide[:, 0:QC]
+        ps[m] = mm(qkv[m, peer_at, :], right, 1, 1)
+        part_copy(PARTS[3], m).start()
+        res[m] += mm(qkv[m, own_at, :], right, 1, 1)
+
+    def ingrad_copy(m):
+        return local(stage.at[m], ingrad_ref.at[m], 11 + 3 * tiles_n + m)
+
+    for m in range(2):
+        qkv_branch(m)
+    sca.pass_on(GUP, 1)
+    for k in range(1, 4):
+        gat.relay(GSUMS, k)
+    for m in range(2):
+        part_copy(PARTS[3], m).wait()
+        stage[m] = res[m] + pr[m]
+        ingrad_copy(m).start()
+    sca.pass_on(GUP, 2)
+    for copy in states:
+        copy.wait()
+
+    one, two = consts[0], consts[1]
+
+    def adam(weight, grad, first, second, anchor):
+        first = BETA_ONE * first + (1.0 - BETA_ONE) * grad
+        second = BETA_TWO * second + (1.0 - BETA_TWO) * grad * grad
+        weight = weight - LEARN_RATE * (
+            (first * one) / (jnp.sqrt(second * two) + ADAM_EPS) + DECAY_RATE * weight
+        )
+        return (anchor - weight).astype(BF16)
+
+    def own_sum(srcs, at):
+        value = srcs[0][:, at].astype(F32) + srcs[1][:, at].astype(F32)
+        value = value + jnp.where(z < ZS - 1, srcs[2][:, at].astype(F32), 0.0)
+        return value + jnp.where(z > 0, srcs[3][:, at].astype(F32), 0.0)
+
+    def y_copy(g):
+        src, dst = (dsn, drn) if g == GNAR else (dsw.at[:, halves(g)], drw.at[:, halves(g)])
+        return pltpu.make_async_remote_copy(
+            src_ref=src, dst_ref=dst, send_sem=ys.at[g], recv_sem=yr.at[g],
+            device_id=near["group"], device_id_type=MESH,
+        )
+
+    def update_wide(g, lo, hi):
+        sca.arrived(g)
+        srcs = (gw.at[span(shard * WR, WR, WR)], xw.at[z], zw.at[z], zw.at[ZS])
+
+        def body(c, _):
+            at = span(c * LANE, LANE, LANE)
+            lin = pl.ds(c, WR, stride=sz.tiles)
+            grad = own_sum(srcs, at)
+            weight = glin[lin, :]
+            dsw[:, at] = adam(
+                weight,
+                grad,
+                *(uu[pl.ds(n * sz.tiles * WR + c, WR, stride=sz.tiles), :] for n in range(3)),
+            )
+            glin[lin, :] = grad
+            return 0
+
+        lax.fori_loop(lo, hi, body, 0)
+        y_copy(g).start()
+
+    def update_narrow(only):
+        @pl.when(only(z))
+        def _():
+            sca.arrived(GNAR)
+            srcs = (gn.at[span(shard * NR, NR, NR)], xn.at[z], zn.at[z], zn.at[ZS])
+
+            def body(c, _):
+                at = span(c * LANE, LANE, LANE)
+                grad = own_sum(srcs, at)
+                gnar[:, at] = grad
+                dsn[:, at] = adam(
+                    wn32[:, at],
+                    grad,
+                    *(uu[span(base + (n * tiles_n + c) * NR, NR, 8), :] for n in range(3)),
+                )
+                return 0
+
+            lax.fori_loop(0, tiles_n, body, 0)
+            y_copy(GNAR).start()
+
+    def mean_wide(g, lo, hi):
+        y_copy(g).wait()
+
+        def body(c, _):
+            at = span(c * LANE, LANE, LANE)
+            mlin[pl.ds(c, WR, stride=sz.tiles), :] = 0.5 * (
+                dsw[:, at].astype(F32) + drw[:, at].astype(F32)
+            )
+            return 0
+
+        lax.fori_loop(lo, hi, body, 0)
+
+    split = QC // LANE
+    update_narrow(other_rows)
+    update_wide(GUP, split, sz.tiles)
+    for k in range(3):
+        sca.pass_on(GNAR, k, first_row)
+    sca.pass_on(GQKV, 0)
+    update_narrow(first_row)
+    sca.pass_on(GQKV, 1)
+
+    gat.across(GSUMS)
+    total = sg_all[0]
+    for s in range(1, 8):
+        total = total + sg_all[s]
+    small_copy().wait_send()
+    sm_mine[...] = total
+
+    def sums_copy():
+        return core_copy(3, sm_mine, sm_peer)
+
+    sums_copy().start()
+    sca.pass_on(GQKV, 2)
+    sums_copy().wait()
+    row_at = lax.broadcasted_iota(jnp.int32, sm_mine.shape, 0)
+    sm_mine[...] += jnp.where(row_at >= nb, sm_peer[...], 0.0)
+    y_copy(GNAR).wait()
+    mnar[...] = 0.5 * (dsn[...].astype(F32) + drn[...].astype(F32))
+    mean_wide(GUP, split, sz.tiles)
+    update_wide(GQKV, 0, split)
+    last = 13 + 3 * tiles_n
+    ends = [
+        local(glin, glin_out, last),
+        local(gnar, gnar_out, last + 1),
+        local(mnar, mnar_out, last + 2),
+        local(sm_mine, small_out, last + 3),
+    ]
+    for copy in ends:
+        copy.start()
+    mean_wide(GQKV, 0, split)
+    tail = local(mlin, mlin_out, last + 4)
+    tail.start()
+
+    for g in range(5):
+        gat.drain(g)
+    for m in range(2):
+        x_copy(m).wait_send()
+        ingrad_copy(m).wait()
+    for g in (GQKV, GUP, GNAR):
+        for k in range(4):
+            sca.drain(g, k)
+    for copy in ends:
+        copy.wait()
+    tail.wait()
+
+
+PARTS = (2, 3, 4, 5)
+ROWS = (6, 7, 8)
+GELU_A = 0.7978845608028654
+GELU_B = 0.044715
 
 
 def gelu_tanh(values):
@@ -172,7 +1018,7 @@
     return (weight_new, first_new, second_new)
 
 
-def on_device(
+def general_path(
     layer_input,
     out_cotangent,
     lengths,
@@ -467,6 +1313,201 @@
         results[3][4],
         results[3][5],
     )
+
+
+def finish_kernel(*refs):
+    for at in (0, 6):
+        grad, mean, first, second, anchor, outer = (ref[...] for ref in refs[at : at + 6])
+        out = refs[12 + at : 18 + at]
+        out[0][...] = grad
+        out[1][...] = BETA_ONE * first + (1.0 - BETA_ONE) * grad
+        out[2][...] = BETA_TWO * second + (1.0 - BETA_TWO) * grad * grad
+        out[3][...] = mean
+        outer_new = OUTER_BETA * outer + mean
+        out[4][...] = outer_new
+        out[5][...] = anchor - OUTER_RATE * (mean + OUTER_BETA * outer_new)
+
+
+def finish(wide_set, narrow_set):
+    steps = 6
+    specs = []
+    for arr in (wide_set[0], narrow_set[0]):
+        rows, cols = arr.shape
+        specs += [pl.BlockSpec((rows // steps, cols), lambda i: (i, 0))] * 6
+    shapes = [jax.ShapeDtypeStruct(arr.shape, F32) for arr in (*wide_set, *narrow_set)]
+    return pl.pallas_call(
+        finish_kernel,
+        grid=(steps,),
+        in_specs=specs,
+        out_specs=specs,
+        out_shape=shapes,
+        name="finish",
+    )(*wide_set, *narrow_set)
+
+
+def fast_path(mesh_sizes, args):
+    (
+        layer_input, out_cotangent, lengths, global_blocks, rand_blocks, inner_steps,
+        wide_inner, wide_first, wide_second, wide_anchor, wide_outer,
+        narrow_inner, narrow_first, narrow_second, narrow_anchor, narrow_outer,
+        bias_inner, bias_first, bias_second, bias_anchor, bias_outer,
+        norms_inner, norms_first, norms_second, norms_anchor, norms_outer,
+    ) = args
+    dp, tensor = lax.axis_index("dp"), lax.axis_index("tensor")
+    x, cot = layer_input[:, 0], out_cotangent[:, 0]
+    rand = jnp.transpose(rand_blocks[:, 0], (0, 2, 3, 1))
+    rand = jnp.pad(rand, ((0, 0), (0, 0), (0, 5), (0, LANE - rand.shape[3])), constant_values=-1)
+
+    def lin(values):
+        return values.reshape(-1, LANE)
+
+    def flat(values):
+        return values.reshape(values.shape[-2:])
+
+    wide_set = [lin(v) for v in (wide_inner, wide_first, wide_second, wide_anchor, wide_outer)]
+    narrow_set = [flat(v) for v in (narrow_inner, narrow_first, narrow_second, narrow_anchor, narrow_outer)]
+    bias_len, rows_len = bias_inner.shape[-1], norms_inner.shape[-1]
+    bias_all, width = bias_len * 8, rows_len * 16
+    count = inner_steps[0].astype(F32)
+    consts = jnp.stack([1.0 / (1.0 - BETA_ONE**count), 1.0 / (1.0 - BETA_TWO**count)])
+    bias_at, rows_at = dp * bias_len, (dp * 2 + tensor) * rows_len
+    bias_low = lax.dynamic_update_slice(
+        jnp.zeros((bias_all,), BF16), bias_inner[0, 0, 0].astype(BF16), (bias_at,)
+    )
+    rows_low = lax.dynamic_update_slice(
+        jnp.zeros((6, width), BF16), norms_inner[0, 0].astype(BF16), (0, rows_at)
+    )
+    small = jnp.concatenate([bias_low.reshape(-1, LANE), rows_low.reshape(-1, LANE)])
+    nb = bias_all // LANE
+    used = small.shape[0]
+    small = jnp.pad(small, ((0, -used % 16), (0, 0)))
+
+    sz = Sizes(x, wide_set[0], narrow_set[0], rand)
+    M, OWN, SEQ, D, DT, FT, WR, NR, WC = sz.micro, sz.own, sz.seq, sz.d, sz.dt, sz.ft, sz.wr, sz.nr, sz.wc
+    vm = pltpu.VMEM
+    deep = DT + FT
+    scratch = [
+        vm((D, WC), BF16),
+        vm((deep, D), BF16),
+        vm((M, SEQ, D), BF16),
+        vm((M, OWN, D), BF16),
+        vm((M, SEQ, 3 * DT), BF16),
+        vm((M * SEQ, DT), BF16),
+        vm((M * SEQ, DT), BF16),
+        vm((M * sz.heads, 8, SEQ), F32),
+        vm((M * sz.heads, SEQ, LANE), BF16),
+        vm((SEQ, LANE), BF16),
+        vm((M, OWN, D), F32),
+        vm((M, OWN, D), F32),
+        vm((M, OWN, D), F32),
+        vm((M, OWN, 1), F32),
+        vm((M * SEQ, D), BF16),
+        vm((FT // LANE * M * SEQ, LANE), F32),
+        vm((M * SEQ, FT), BF16),
+        vm((M * SEQ, D), BF16),
+        vm((M, OWN, D), F32),
+        vm((M, OWN, D), F32),
+        vm((D, WC), BF16),
+        vm((deep, D), BF16),
+        vm((ZS, WR, WC), BF16),
+        vm((ZS, NR, D), BF16),
+        vm((ZS + 1, WR, WC), BF16),
+        vm((ZS + 1, NR, D), BF16),
+        vm((sz.tiles * WR, LANE), F32),
+        vm((NR, D), F32),
+        vm((sz.tiles * WR, LANE), F32),
+        vm((NR, D), F32),
+        vm((NR, D), F32),
+        vm((WR, WC), BF16),
+        vm((NR, D), BF16),
+        vm((WR, WC), BF16),
+        vm((NR, D), BF16),
+        vm((8, *small.shape), BF16),
+        vm((8, *small.shape), F32),
+        vm(small.shape, F32),
+        vm(small.shape, F32),
+        vm((8, bias_all), F32),
+        vm((8, D), F32),
+        vm((8, bias_all), F32),
+        vm((6, 8, D), F32),
+        DMA((5, ZS, 3)),
+        DMA((5, 8)),
+        DMA((3, ZS)),
+        DMA((3, ZS)),
+        DMA((3, ZS)),
+        DMA((3, ZS + 1)),
+        DMA((18,)),
+        DMA((18,)),
+        DMA((3,)),
+        DMA((3,)),
+        DMA((18 + 3 * (D // LANE),)),
+    ]
+    shape = jax.ShapeDtypeStruct
+    lin_shape, flat_shape = shape((sz.tiles * WR, LANE), F32), shape((NR, D), F32)
+    layer_out, input_grad, glin, gnar, mlin, mnar, sums = pl.pallas_call(
+        lambda *refs: layer_kernel(sz, *refs),
+        out_shape=(
+            shape((M, OWN, D), F32), shape((M, OWN, D), F32),
+            lin_shape, flat_shape, lin_shape, flat_shape, shape(small.shape, F32),
+        ),
+        in_specs=[
+            ANY_SPEC, ANY_SPEC, SMEM_SPEC, SMEM_SPEC, VMEM_SPEC, SMEM_SPEC, VMEM_SPEC,
+            *([ANY_SPEC] * 8),
+        ],
+        out_specs=(ANY_SPEC,) * 7,
+        scratch_shapes=scratch,
+        compiler_params=pltpu.CompilerParams(
+            collective_id=1, has_side_effects=True, vmem_limit_bytes=BIG_VMEM
+        ),
+        name="layer_step",
+    )(
+        x, cot, lengths[:, 0], global_blocks[:, 0], rand, consts, small,
+        wide_set[0], narrow_set[0], *wide_set[1:4], *narrow_set[1:4],
+    )
+
+    done = finish((glin, mlin, *wide_set[1:5]), (gnar, mnar, *narrow_set[1:5]))
+
+    bias_grad = lax.dynamic_slice(sums[:nb].reshape(-1), (bias_at,), (bias_len,))
+    rows_grad = lax.dynamic_slice(sums[nb:used].reshape(6, width), (0, rows_at), (6, rows_len))
+    results = []
+    for grad, inner, first, second, anchor, outer in (
+        (bias_grad, bias_inner, bias_first, bias_second, bias_anchor, bias_outer),
+        (rows_grad, norms_inner, norms_first, norms_second, norms_anchor, norms_outer),
+    ):
+        grad = grad.reshape(inner.shape)
+        weight, first_new, second_new = adam_step(inner, grad, first, second, count)
+        results.append([grad, first_new, second_new, anchor - weight[0], anchor, outer])
+    sent = [item[3] for item in results]
+    sums_of = lax.psum(tuple(sent), "group")
+    smalls = []
+    for item, total in zip(results, sums_of):
+        mean_diff = total / 2
+        outer_new = OUTER_BETA * item[5] + mean_diff
+        anchor_new = item[4] - OUTER_RATE * (mean_diff + OUTER_BETA * outer_new)
+        smalls += [item[0], item[1], item[2], mean_diff, outer_new, anchor_new]
+    like = lambda values, kinds: [v.reshape(k.shape) for v, k in zip(values, kinds)]
+    wide_out = like(done[:6], [wide_inner] * 3 + [wide_anchor] * 3)
+    narrow_out = like(done[6:], [narrow_inner] * 3 + [narrow_anchor] * 3)
+    return (layer_out[:, None], input_grad[:, None], *wide_out, *narrow_out, *smalls)
+
+
+def on_device(*args):
+    layer_input, rand_blocks, wide_inner, narrow_inner = args[0], args[4], args[6], args[11]
+    heads, tokens, width = rand_blocks.shape[3], layer_input.shape[2], layer_input.shape[3]
+    fits = (
+        (lax.axis_size("dp"), lax.axis_size("tensor"), lax.axis_size("group")) == (8, 2, 2)
+        and layer_input.shape[:2] == (2, 1)
+        and wide_inner.shape[1] == 1
+        and rand_blocks.shape[2] == 8
+        and tokens == 256
+        and width == heads * 2 * 64
+        and heads % 2 == 0
+        and wide_inner.shape[4] == 3 * heads * 64 + 2 * width
+        and wide_inner.shape[2] % 48 == 0
+        and narrow_inner.shape[3] % 48 == 0
+        and width % 256 == 0
+    )
+    return fast_path(None, args) if fits else general_path(*args)
 
 
 def solution(mesh):

time: 799 us -> 240 us (0.30)
  waiting for transfers between devices: 497 us -> 0 us
  Pallas kernels: 0 us -> 220 us
  matrix products: 92.2 us -> 0 us
  blocking collectives: 68.5 us -> 4.96 us
  other arithmetic: 66.5 us -> 5.09 us
  local copies, waits for them, and re-layouts: 48.2 us -> 8.14 us
  between operations: 17.4 us -> 1.63 us
    reduce_scatter x10 -> x0, waiting for transfers between devices: 283 us -> none  [the longest x1 147 us: on_device(): lax.psum_scatter(merged[0], 'dp', scatter_dimension=1, tiled=True)]
    pallas_call x0 -> x2, Pallas kernels: none -> 220 us  [the longest x1 210 us: fast_path(): pl.pallas_call(lambda *refs: layer_kernel(sz, *refs), out_shape=(shape((M...]
    all_gather x2 -> x0, waiting for transfers between devices: 95.8 us -> none  [the longest x1 50.4 us: on_device(): lax.all_gather(narrow_inner[0, 0, 0].astype(jnp.bfloat16), 'dp', axis=0,...]
    dot_general x36 -> x0, matrix products: 92.2 us -> none  [the longest x2 9.76 us: on_device(): jnp.einsum('sf,sd->fd', gelu_out, full_two, preferred_element_type=jnp.fl...]
    unnamed x17 -> x0, waiting for transfers between devices: 67.1 us -> none
    psum x1 -> x0, waiting for transfers between devices: 52.1 us -> none  [on_device(): diff_sums = lax.psum((diffs[0], diffs[1], diffs[2], diffs[3]), 'group')]
    all_gather x9 -> x0, blocking collectives: 39.7 us -> none  [the longest x1 20.1 us: on_device(): lax.all_gather(norms_inner[0].astype(jnp.bfloat16), ('dp', 'tensor'), axi...]
    unnamed x245 -> x29, local copies, waits for them, and re-layouts: 37.6 us -> 4.49 us
  transfers between devices with their start and end apart: 15 -> 0, of which waited for: 10 -> 0; matrix products, arithmetic and copies ran while one was open for 16% -> 0% of each run, Pallas kernels for 0% -> 0%
where the time goes in v2:
time: 240 us
  Pallas kernels  220 us (92%)
  local copies, waits for them, and re-layouts  8.14 us (3%)
  other arithmetic  5.09 us (2%)
  blocking collectives  4.96 us (2%)
    pallas_call x1, Pallas kernels, fast_path(): pl.pallas_call(lambda *refs: layer_kernel(sz, *refs), out_shape=(shape((M...  210 us
    pallas_call x1, Pallas kernels, finish(): pl.pallas_call(finish_kernel, grid=(steps,), in_specs=specs, out_specs=sp...  9.42 us
    psum x1, blocking collectives, fast_path(): sums_of = lax.psum(tuple(sent), 'group')  4.96 us

profile of v2, /device:TPU:0, one launch (start us, length us, event | category | flops | bytes accessed | tf_op | source)
XLA Modules:
  0.0 239.5 jit_solution(17234318887430224165)
XLA Ops:
  1.5 0.6 pad_maximum_fusion.refs_5_
  2.1 0.7 convert_reduce_fusion
  2.8 0.7 convert_element_type.21
  3.5 0.3 dynamic_update_slice.6
  3.7 0.1 dynamic_update_slice.7
  3.9 0.6 fusion.2.refs_6_
  4.5 0.7 copy.93
  5.3 0.6 pad.8.refs_4_
  5.9 0.0 copy-start.4
  5.9 0.0 copy-start.5
  5.9 0.0 copy-start.10
  5.9 0.0 copy-start.11
  5.9 0.0 copy-start.8
  5.9 0.0 copy-start.2
  5.9 0.0 copy-start.3
  5.9 0.0 copy-start.6
  6.0 0.0 copy-start.9
  6.0 0.0 copy-start.7
  6.0 210.3 %layer_step.1 = (f32[2,256,768]{2,1,0:T(8,128)}, f32[2,256,768]{2,1,0:T(8,128)}, f32[2016,128]{1,0:T(8,128)}, f32[240,768]{1,0:T(8,128)}, f32[2016,128]{1,0:T(8,...) custom-call(bf16[2,256,768]{2,1,0:T(8,128)(2,1)} %bitcast.93, bf16[2,256,768]{2,1,0:T(8,128)(2,1)} %bitcast.94, s32[2]{0:T(128)} %bitcast.102, ...), custom_call_target="tpu_custom_call" | custom-call | tf_op jit(solution)/shard_map/layer_step/pallas_call | solution.py:1447
  216.3 0.7 slice_bitcast_fusion
  217.0 0.7 slice.7
  217.7 0.1 multiply_multiply_fusion.1
  217.8 0.6 reshape.178
  218.4 0.0 copy-done.4
  218.4 0.0 copy-done.5
  218.4 0.0 copy-done.10
  218.4 0.0 copy-done.11
  218.4 0.6 bitcast_subtract_fusion.2
  219.0 0.0 copy-done.8
  219.0 0.1 bitcast_add_fusion
  219.0 0.6 copy.81
  219.6 0.6 reshape.180
  220.2 0.0 copy-done.2
  220.2 0.0 copy-done.3
  220.2 0.0 copy-done.6
  220.2 0.6 bitcast_subtract_fusion
  220.8 5.0 %all-reduce.2 = (f32[1,1,288]{2,1,0:T(1,128)S(1)}, f32[1,6,48]{2,0,1:T(1,128)S(1)}) all-reduce(f32[1,1,288]{2,1,0:T(1,128)S(1)} %get-tuple-element.128, f32[1,6,48]{2,0,1:T(1,128)S(1)} %get-tuple-element.124), channel_id=1, replica_groups=mesh['group'=2,'dp'=8,'tensor'=2] {'group'}, use_global_device_ids=true, to_apply=%region_0.1 | all-reduce | flops 576 | bytes 4608 | tf_op jit(solution)/shard_map/psum | solution.py:1481
  225.8 0.0 copy-done.9
  225.8 0.6 multiply_subtract_fusion.1
  226.4 0.0 copy-done.7
  226.4 0.6 multiply_subtract_fusion
  227.0 0.0 copy-start.1
  227.0 9.4 %finish.1 = (f32[2016,128]{1,0:T(8,128)}, f32[2016,128]{1,0:T(8,128)}, f32[2016,128]{1,0:T(8,128)}, f32[2016,128]{1,0:T(8,128)}, f32[2016,128]{1,0:T(8,128)}, /*...) custom-call(f32[2016,128]{1,0:T(8,128)} %get-tuple-element.47.refs_0, ...), custom_call_target="tpu_custom_call" | custom-call | tf_op jit(solution)/shard_map/finish/pallas_call | solution.py:1338
  236.4 0.0 copy-done.1
  236.4 0.0 copy-start
  236.4 1.1 copy.100
  237.5 0.8 copy-done
  238.4 1.1 copy.101
  (8 shorter events, 0.1 us)
Async XLA Ops:
  5.9 212.5 %copy-start.4 = (f32[1,1,288]{2,1,0:T(1,128)S(1)}, f32[1,1,288]{2,1,0:T(1,128)}, u32[]{:S(2)}) copy-start(f32[1,1,288]{2,1,0:T(1,128)} %param.45) | copy-start | bytes 3460
  5.9 212.5 %copy-start.5 = (f32[1,1,1,288]{3,2,1,0:T(1,128)S(1)}, f32[1,1,1,288]{3,2,1,0:T(1,128)}, u32[]{:S(2)}) copy-start(f32[1,1,1,288]{3,2,1,0:T(1,128)} %param.42) | copy-start | bytes 3460
  5.9 212.5 %copy-start.10 = (f32[1,1,1,288]{3,2,1,0:T(1,128)S(1)}, f32[1,1,1,288]{3,2,1,0:T(1,128)}, u32[]{:S(2)}) copy-start(f32[1,1,1,288]{3,2,1,0:T(1,128)} %param.44) | copy-start | bytes 3460
  5.9 212.5 %copy-start.11 = (f32[1,1,1,288]{3,2,1,0:T(1,128)S(1)}, f32[1,1,1,288]{3,2,1,0:T(1,128)}, u32[]{:S(2)}) copy-start(f32[1,1,1,288]{3,2,1,0:T(1,128)} %param.43) | copy-start | bytes 3460
  5.9 213.1 %copy-start.8 = (f32[1,1,6,48]{3,1,2,0:T(1,128)S(1)}, f32[1,1,6,48]{3,1,2,0:T(1,128)}, u32[]{:S(2)}) copy-start(f32[1,1,6,48]{3,1,2,0:T(1,128)} %param.48) | copy-start | bytes 3460
  5.9 214.3 %copy-start.2 = (f32[1,6,48]{2,0,1:T(1,128)S(1)}, f32[1,6,48]{2,0,1:T(1,128)}, u32[]{:S(2)}) copy-start(f32[1,6,48]{2,0,1:T(1,128)} %param.50) | copy-start | bytes 3460
  5.9 214.3 %copy-start.3 = (f32[1,1,6,48]{3,1,2,0:T(1,128)S(1)}, f32[1,1,6,48]{3,1,2,0:T(1,128)}, u32[]{:S(2)}) copy-start(f32[1,1,6,48]{3,1,2,0:T(1,128)} %param.47) | copy-start | bytes 3460
  5.9 214.3 %copy-start.6 = (f32[1,1,6,48]{3,1,2,0:T(1,128)S(1)}, f32[1,1,6,48]{3,1,2,0:T(1,128)}, u32[]{:S(2)}) copy-start(f32[1,1,6,48]{3,1,2,0:T(1,128)} %param.49) | copy-start | bytes 3460
  6.0 219.8 %copy-start.9 = (f32[1,1,288]{2,1,0:T(1,128)S(1)}, f32[1,1,288]{2,1,0:T(1,128)}, u32[]{:S(2)}) copy-start(f32[1,1,288]{2,1,0:T(1,128)} %param.46) | copy-start | bytes 3460
  6.0 220.4 %copy-start.7 = (f32[1,6,48]{2,0,1:T(1,128)S(1)}, f32[1,6,48]{2,0,1:T(1,128)}, u32[]{:S(2)}) copy-start(f32[1,6,48]{2,0,1:T(1,128)} %param.51) | copy-start | bytes 3460
  227.0 9.4 %copy-start.1 = (f32[2,256,768]{2,1,0:T(8,128)S(1)}, f32[2,256,768]{2,1,0:T(8,128)}, u32[]{:S(2)}) copy-start(f32[2,256,768]{2,1,0:T(8,128)} %get-tuple-element.45) | copy-start | bytes 4718596
  236.4 2.0 copy-start
